TPU v7x, 32 devices: a whole 2x2x4 slice. The times are simulated.
32 devices in a mesh: dp: 4 (over y, x), tensor: 8 (over z, core).
Axes of the slice: x: 2, y: 2, z: 4, core: 2. Of those that a mesh axis runs over, the one named last changes fastest.
Arguments:
- tokens: bfloat16 [1536, 8192], P('dp', 'tensor'), may hold values from -6 to 6
- cotangent: bfloat16 [1536, 8192], P('dp', 'tensor'), may hold values from -6 to 6
- gate_weight: bfloat16 [8192, 14336], P(None, 'tensor'), may hold values from -0.09375 to 0.09375
- up_weight: bfloat16 [8192, 14336], P(None, 'tensor'), may hold values from -0.09375 to 0.09375
- down_weight: bfloat16 [14336, 8192], P('tensor'), may hold values from -0.0625 to 0.0625
- block_task: int32 [12], P('dp'), may hold values from 0 to 63
- block_fill: int32 [12], P('dp'), may hold values from 1 to 128
- task_slot: int32 [64], replicated, may hold values from 0 to 63, each once
- inner_correction_weights: bfloat16 [64, 64, 8192], P('dp', None, 'tensor'), may hold values from -0.0625 to 0.0625
- up_b: bfloat16 [64, 64, 14336], P('dp', None, 'tensor'), may hold values from -0.75 to 0.75
Outputs:
- mixed: bfloat16 [1536, 8192], P('dp', 'tensor')
- item_derivative: bfloat16 [1536, 8192], P('dp', 'tensor')
- up_a_grad: bfloat16 [64, 64, 8192], P('dp', None, 'tensor')
- up_b_grad: bfloat16 [64, 64, 14336], P('dp', None, 'tensor')
Inputs may be any that keep to these rules, and one draw needn't show every extreme that they name: `task_slot`: slot s is held by data group s // 16.
All inputs are finite; a program needn't handle non-finite values.
Results may differ from a plain program's by a relative error of at most 0.019.
Values may be sent and summed in bfloat16 or wider, within the bound.
No kernel may reach another device: no remote copies, remote signals or barrier semaphores. Data moves between devices by JAX's collectives and lax.ppermute only.
A program may use at most 192 MiB of HBM per device.

v0:
```python
import jax
import jax.numpy as jnp
from jax import lax
from jax.sharding import PartitionSpec as P

BLOCK = 128


adapter_scale = 0.25


def tensor_total(value):
    return lax.psum(value.astype(jnp.bfloat16), "tensor").astype(jnp.float32)


def common_result(value):
    return lax.psum_scatter(
        value.astype(jnp.bfloat16), "tensor", scatter_dimension=1, tiled=True
    ).astype(jnp.float32)


def body(
    tokens,
    cotangent,
    gate_weight,
    up_weight,
    down_weight,
    block_task,
    block_fill,
    task_slot,
    inner_correction_weights,
    up_b,
):
    row_count, local_width = tokens.shape
    block_count = block_task.shape[0]
    slot_dev = inner_correction_weights.shape[0]
    hidden_width = gate_weight.shape[1]
    task_ids = jnp.arange(task_slot.shape[0], dtype=jnp.int32)
    segment_owner_index = jnp.sum(
        jnp.where(block_task[:, None] == task_ids[None, :], task_slot[None, :], 0), axis=1
    )
    enabled_flags = (jnp.arange(BLOCK, dtype=jnp.int32)[None, :] < block_fill[:, None]).astype(
        jnp.float32
    )[..., None]
    block_ids = jnp.arange(block_count, dtype=jnp.int32)
    holder = segment_owner_index // slot_dev
    kept_position = segment_owner_index - holder * slot_dev
    peer_ids = jnp.arange(lax.axis_size("dp"), dtype=jnp.int32)
    chosen = holder[None, :] == peer_ids[:, None]
    request = jnp.where(chosen, kept_position[None, :], -1)
    asked = lax.all_to_all(request, "dp", split_axis=0, concat_axis=0, tiled=True)
    safe = jnp.maximum(asked, 0)
    reply_in = lax.all_to_all(
        inner_correction_weights[safe], "dp", split_axis=0, concat_axis=0, tiled=True
    )
    reply_out = lax.all_to_all(up_b[safe], "dp", split_axis=0, concat_axis=0, tiled=True)
    correction_source_vector = reply_in[holder, block_ids]
    up_factor_output = reply_out[holder, block_ids]
    piece = lax.all_gather(tokens, "tensor", axis=1, tiled=True)
    gating_piece = jnp.dot(piece, gate_weight, preferred_element_type=jnp.float32)
    expansion_running_total = jnp.dot(piece, up_weight, preferred_element_type=jnp.float32)
    d_hidden = lax.dot_general(
        lax.all_gather(cotangent, "tensor", axis=1, tiled=True),
        down_weight,
        (((1,), (1,)), ((), ())),
        preferred_element_type=jnp.float32,
    )
    portion_clusters = tokens.reshape(block_count, BLOCK, local_width)
    narrow_product = (
        tensor_total(
            jnp.einsum(
                "imk,iok->imo",
                portion_clusters,
                correction_source_vector,
                preferred_element_type=jnp.float32,
            )
        )
        * enabled_flags
    )
    low_rank_b_output = narrow_product.astype(jnp.bfloat16)
    adapter_up_output = jnp.einsum(
        "vam,vmk->vak", low_rank_b_output, up_factor_output, preferred_element_type=jnp.float32
    ).reshape(row_count, hidden_width)
    up_projection = expansion_running_total + adapter_scale * adapter_up_output
    sigmoid_gate = jax.nn.sigmoid(gating_piece)
    activated = gating_piece * sigmoid_gate
    hidden = (activated * up_projection).astype(jnp.bfloat16)
    mixed = common_result(jnp.dot(hidden, down_weight, preferred_element_type=jnp.float32)).astype(
        jnp.bfloat16
    )
    d_gate = (
        d_hidden * up_projection * sigmoid_gate * (1.0 + gating_piece * (1.0 - sigmoid_gate))
    ).astype(jnp.bfloat16)
    d_up = (d_hidden * activated).astype(jnp.bfloat16)
    gradient_per_block = d_up.reshape(block_count, BLOCK, hidden_width)
    narrow_derivative = (
        adapter_scale
        * tensor_total(
            jnp.einsum(
                "oge,oce->ogc",
                gradient_per_block,
                up_factor_output,
                preferred_element_type=jnp.float32,
            )
        )
        * enabled_flags
    )
    exterior_multiplier_dual = narrow_derivative.astype(jnp.bfloat16)
    contract = (((1,), (1,)), ((), ()))
    fixed_weight_derivative = lax.dot_general(
        d_gate, gate_weight, contract, preferred_element_type=jnp.float32
    )
    fixed_weight_derivative = fixed_weight_derivative + lax.dot_general(
        d_up, up_weight, contract, preferred_element_type=jnp.float32
    )
    adjoint_of_correction = jnp.einsum(
        "lxu,luz->lxz",
        exterior_multiplier_dual,
        correction_source_vector,
        preferred_element_type=jnp.float32,
    ).reshape(row_count, local_width)
    item_derivative = (common_result(fixed_weight_derivative) + adjoint_of_correction).astype(
        jnp.bfloat16
    )
    arriving_slope = jnp.einsum(
        "bqf,bqm->bfm",
        exterior_multiplier_dual,
        portion_clusters,
        preferred_element_type=jnp.float32,
    )
    output_gradient = adapter_scale * jnp.einsum(
        "wvd,wvg->wdg", low_rank_b_output, gradient_per_block, preferred_element_type=jnp.float32
    )
    outgoing_in = jnp.where(chosen[:, :, None, None], arriving_slope[None], 0.0)
    outgoing_out = jnp.where(chosen[:, :, None, None], output_gradient[None], 0.0)
    back_in, returned_cotangent = (
        lax.all_to_all(
            outgoing_in.astype(jnp.bfloat16), "dp", split_axis=0, concat_axis=0, tiled=True
        ).astype(outgoing_in.dtype),
        lax.all_to_all(
            outgoing_out.astype(jnp.bfloat16), "dp", split_axis=0, concat_axis=0, tiled=True
        ).astype(outgoing_out.dtype),
    )
    resident_task_places = jnp.arange(slot_dev, dtype=jnp.int32)
    match = (asked[:, :, None] == resident_task_places[None, None, :]).astype(jnp.float32)
    owned_in = jnp.einsum("qbs,qbrd->srd", match, back_in, precision=lax.Precision.HIGHEST)
    owned_out = jnp.einsum(
        "qbs,qbrf->srf", match, returned_cotangent, precision=lax.Precision.HIGHEST
    )
    return (mixed, item_derivative, owned_in.astype(jnp.bfloat16), owned_out.astype(jnp.bfloat16))


def solution(mesh):
    return jax.shard_map(
        body,
        mesh=mesh,
        in_specs=(
            P("dp", "tensor"),
            P("dp", "tensor"),
            P(None, "tensor"),
            P(None, "tensor"),
            P("tensor", None),
            P("dp"),
            P("dp"),
            P(),
            P("dp", None, "tensor"),
            P("dp", None, "tensor"),
        ),
        out_specs=(
            P("dp", "tensor"),
            P("dp", "tensor"),
            P("dp", None, "tensor"),
            P("dp", None, "tensor"),
        ),
        check_vma=False,
    )
```

profile of v0, /device:TPU:0, one launch (start us, length us, event | category | flops | bytes accessed | tf_op | source)
XLA Modules:
  0.0 430.5 jit_solution(9149227730486260911)
XLA Ops:
  10.1 9.6 %all_to_all.26 = s32[4,1,3]{2,1,0:T(1,128)S(1)} all-to-all(s32[4,1,3]{2,1,0:T(1,128)S(1)} %compare_select_fusion), channel_id=1, replica_groups=mesh['dp'=4,'tensor'=8] {'dp'}, dimensions={0} | all-to-all | bytes 96 | tf_op jit(solution)/shard_map/all_to_all | solution.py:51
  20.4 1.8 gather_fusion
  22.3 3.6 all-to-all-start.1
  25.8 4.4 %gather_fusion.2 = bf16[12,64,1792]{2,1,0:T(8,128)(2,1)} fusion(bf16[16,64,1792]{2,1,0:T(8,128)(2,1)} %param.19, s32[1024]{0:T(1024)S(1)} %pad_clamp_fusion), kind=kCustom, calls=%fused_computation.2 | custom fusion | bytes 5505072 | tf_op jit(solution)/shard_map/gather | solution.py:56
  30.3 13.6 %all-to-all-done.1 = bf16[4,3,64,1024]{3,2,1,0:T(8,128)(2,1)S(1)} async-done(((bf16[4,3,64,1024]{3,2,1,0:T(8,128)(2,1)}), bf16[4,3,64,1024]{3,2,1,0:T(8,128)(2,1)S(1)}, u32[]{:S(2)}, u32[]{:S(2)}) %all-to-all-start.1) | async-done | bytes 1572896 | tf_op jit(solution)/shard_map/all_to_all | solution.py:53
  45.0 4.8 %all-to-all-start.2 = ((bf16[4,3,64,1792]{3,2,1,0:T(8,128)(2,1)}), bf16[4,3,64,1792]{3,2,1,0:T(8,128)(2,1)}, u32[]{:S(2)}, u32[]{:S(2)}) async-start(bf16[4,3,64,1792]{3,2,1,0:T(8,128)(2,1)} %bitcast.5), calls=%async_computation.2 | async-start | bytes 5505024 | tf_op jit(solution)/shard_map/all_to_all | solution.py:56
  49.9 2.0 gather_fusion.1
  52.9 28.4 %all-to-all-done.2 = bf16[4,3,64,1792]{3,2,1,0:T(8,128)(2,1)} async-done(((bf16[4,3,64,1792]{3,2,1,0:T(8,128)(2,1)}), bf16[4,3,64,1792]{3,2,1,0:T(8,128)(2,1)}, u32[]{:S(2)}, u32[]{:S(2)}) %all-to-all-start.2) | async-done | bytes 2752544 | tf_op jit(solution)/shard_map/all_to_all | solution.py:56
  81.3 2.4 gather_fusion.3
  83.7 20.2 %fusion.23 = f32[384,1792]{1,0:T(8,128)} fusion(bf16[384,8192]{1,0:T(8,128)(2,1)} %all-gather.3.cloned.1.call-done, bf16[8192,1792]{1,0:T(8,128)(2,1)} %param.12), kind=kOutput, calls=%fused_computation.61 | convolution fusion | flops 11274289152 | bytes 38404096 | tf_op jit(solution)/shard_map/dot_general | solution.py:60
  103.9 38.2 %all-gather.5.cloned.1.call-done = bf16[384,8192]{1,0:T(8,128)(2,1)} async-done(((bf16[384,1024]{1,0:T(8,128)(2,1)}), bf16[384,8192]{1,0:T(8,128)(2,1)}) %all-gather.5.cloned.1.call-update) | async-done | bytes 6291472 | tf_op jit(solution)/shard_map/all_gather | solution.py:63
  142.1 22.2 %multiply_convert_fusion = (bf16[384,1792]{1,0:T(8,128)(2,1)S(1)}, f32[384,1792]{1,0:T(8,128)}) fusion(f32[384,1792]{1,0:T(8,128)} %fusion.23, bf16[384,8192]{1,0:T(8,128)(2,1)} %all-gather.5.cloned.1.call-done, bf16[1792,8192]{1,0:T(8,128)(2,1)} %param.14), kind=kOutput, calls=%fused_computation.13 | convolution fusion | flops 11278417920 | bytes 42532864 | tf_op jit(solution)/shard_map/dot_general | solution.py:62
  164.3 1.2 convolution_convert_fusion.1
  165.7 50.6 %all-reduce.3.cloned.1.call-done = (bf16[3,128,64]{1,2,0:T(8,128)(2,1)}, bf16[3,128,64]{1,2,0:T(8,128)(2,1)}) async-done(((bf16[3,128,64]{1,2,0:T(8,128)(2,1)}, bf16[3,128,64]{1,2,0:T(8,128)(2,1)}), (bf16[3,128,64]{1,2,0:T(8,128)(2,1)}, bf16[3,128,64]{1,2,0:T(8,128)(2,1)})) %all-reduce.3.cloned.1.call-update) | async-done | bytes 98320 | tf_op jit(solution)/shard_map/psum | solution.py:13
  216.3 1.4 convolution_multiply_fusion
  217.6 19.9 %convolution_add_fusion = f32[384,1792]{1,0:T(8,128)} fusion(f32[384,1792]{1,0:T(8,128)S(1)} %bitcast.57, bf16[384,8192]{1,0:T(8,128)(2,1)} %all-gather.3.cloned.1.call-done, bf16[8192,1792]{1,0:T(8,128)(2,1)} %param.13), kind=kOutput, calls=%fused_computation.11 | convolution fusion | flops 11274977280 | bytes 41156608 | tf_op jit(solution)/shard_map/dot_general | solution.py:61
  237.6 22.7 %fusion.4 = f32[384,8192]{1,0:T(8,128)} fusion(bf16[8192,1792]{1,0:T(8,128)(2,1)} %param.12, f32[384,1792]{1,0:T(8,128)} %fusion.23, f32[384,1792]{1,0:T(8,128)} %get-tuple-element.29, f32[384,1792]{1,0:T(8,128)} %convolution_add_fusion), kind=kOutput, calls=%fused_computation.22 | convolution fusion | flops 11281170432 | bytes 50200576 | tf_op jit(solution)/shard_map/dot_general | solution.py:110
  260.3 21.0 %add_convert_fusion = bf16[384,8192]{1,0:T(8,128)(2,1)} fusion(f32[384,8192]{1,0:T(8,128)} %fusion.4, bf16[384,1792]{1,0:T(8,128)(2,1)S(1)} %get-tuple-element.28, bf16[8192,1792]{1,0:T(8,128)(2,1)} %param.13), kind=kOutput, calls=%fused_computation.4 | convolution fusion | flops 11280580608 | bytes 49610752 | tf_op jit(solution)/shard_map/dot_general | solution.py:113
  281.4 30.5 %convolution_convert_fusion = bf16[384,8192]{1,0:T(8,128)(2,1)} fusion(bf16[1792,8192]{1,0:T(8,128)(2,1)} %param.14, f32[384,1792]{1,0:T(8,128)} %convolution_add_fusion, f32[384,1792]{1,0:T(8,128)} %fusion.23), kind=kOutput, calls=%fused_computation.5 | convolution fusion | flops 11281563648 | bytes 41156608 | tf_op jit(solution)/shard_map/dot_general | solution.py:88
  313.3 1.5 select_convert_fusion.1
  314.9 4.4 %all-to-all-start.3 = ((bf16[4,3,64,1024]{3,2,1,0:T(8,128)(2,1)}), bf16[4,3,64,1024]{3,2,1,0:T(8,128)(2,1)}, u32[]{:S(2)}, u32[]{:S(2)}) async-start(bf16[4,3,64,1024]{3,2,1,0:T(8,128)(2,1)} %select_convert_fusion.1), calls=%async_computation.5 | async-start | bytes 3145728 | tf_op jit(solution)/shard_map/all_to_all | solution.py:137
  319.6 2.1 select_convert_fusion
  321.7 16.5 %all-to-all-done.3 = bf16[4,3,64,1024]{3,2,1,0:T(8,128)(2,1)} async-done(((bf16[4,3,64,1024]{3,2,1,0:T(8,128)(2,1)}), bf16[4,3,64,1024]{3,2,1,0:T(8,128)(2,1)}, u32[]{:S(2)}, u32[]{:S(2)}) %all-to-all-start.3) | async-done | bytes 1572896 | tf_op jit(solution)/shard_map/all_to_all | solution.py:137
  338.2 4.6 %all-to-all-start.4 = ((bf16[4,3,64,1792]{3,2,1,0:T(8,128)(2,1)}), bf16[4,3,64,1792]{3,2,1,0:T(8,128)(2,1)}, u32[]{:S(2)}, u32[]{:S(2)}) async-start(bf16[4,3,64,1792]{3,2,1,0:T(8,128)(2,1)} %select_convert_fusion), calls=%async_computation.6 | async-start | bytes 5505024 | tf_op jit(solution)/shard_map/all_to_all | solution.py:140
  342.9 1.5 fusion.9
  344.4 3.4 bitcast_convert_fusion.1
  347.9 2.5 copy.35
  350.3 23.8 %all-to-all-done.4 = bf16[4,3,64,1792]{3,2,1,0:T(8,128)(2,1)} async-done(((bf16[4,3,64,1792]{3,2,1,0:T(8,128)(2,1)}), bf16[4,3,64,1792]{3,2,1,0:T(8,128)(2,1)}, u32[]{:S(2)}, u32[]{:S(2)}) %all-to-all-start.4) | async-done | bytes 2752544 | tf_op jit(solution)/shard_map/all_to_all | solution.py:140
  374.2 7.0 %bitcast_convert_fusion = bf16[16,64,1792]{2,0,1:T(8,128)(2,1)S(1)} fusion(bf16[4,3,64,1792]{3,2,1,0:T(8,128)(2,1)} %all-to-all-done.4, s32[4,3]{0,1:T(4,128)S(1)} %copy.32), kind=kOutput, calls=%fused_computation.6 | convolution fusion | flops 45875392 | bytes 6422576 | tf_op jit(solution)/shard_map/qbs,qbrf->srf/dot_general | solution.py:147
  381.2 2.9 copy.36
  384.1 2.7 fusion.2
  386.8 37.0 %reduce-scatter.3.cloned.1.call-done = bf16[384,1024]{1,0:T(8,128)(2,1)} async-done(((bf16[384,8192]{1,0:T(8,128)(2,1)}), bf16[384,1024]{1,0:T(8,128)(2,1)}) %reduce-scatter.3.cloned.1.call-update) | async-done | bytes 786448 | tf_op jit(solution)/shard_map/reduce_scatter | solution.py:17
  (54 shorter events, 7.9 us)
Async XLA Ops:
  7.2 13.3 %copy-start = (bf16[16,64,1024]{2,1,0:T(8,128)(2,1)S(1)}, bf16[16,64,1024]{2,1,0:T(8,128)(2,1)}, u32[]{:S(2)}) copy-start(bf16[16,64,1024]{2,1,0:T(8,128)(2,1)} %param.18) | copy-start | bytes 6291460
  7.2 76.5 %all-gather.3.cloned.1.call-start = ((), (), s32[]{:S(2)}) async-start(), calls=%async_computation.7 | async-start | bytes 7077888 | tf_op jit(solution)/shard_map/all_gather | solution.py:59
  7.9 134.2 %all-gather.5.cloned.1.call-start = ((), (), s32[]{:S(2)}) async-start(), calls=%async_computation.9 | async-start | bytes 7077888 | tf_op jit(solution)/shard_map/all_gather | solution.py:63
  9.5 0.6 copy-start.12
  19.7 0.6 copy-start.9
  22.3 21.6 %all-to-all-start.1 = ((bf16[4,3,64,1024]{3,2,1,0:T(8,128)(2,1)}), bf16[4,3,64,1024]{3,2,1,0:T(8,128)(2,1)S(1)}, u32[]{:S(2)}, u32[]{:S(2)}) async-start(bf16[4,3,64,1024]{3,2,1,0:T(8,128)(2,1)} %bitcast.54), calls=%async_computation.1 | async-start | bytes 3145728 | tf_op jit(solution)/shard_map/all_to_all | solution.py:53
  43.9 1.1 copy-start.6
  45.0 6.8 %copy-start.2 = (bf16[384,1024]{1,0:T(8,128)(2,1)S(1)}, bf16[384,1024]{1,0:T(8,128)(2,1)}, u32[]{:S(2)}) copy-start(bf16[384,1024]{1,0:T(8,128)(2,1)} %param.10) | copy-start | bytes 2359300
  45.0 36.3 %all-to-all-start.2 = ((bf16[4,3,64,1792]{3,2,1,0:T(8,128)(2,1)}), bf16[4,3,64,1792]{3,2,1,0:T(8,128)(2,1)}, u32[]{:S(2)}, u32[]{:S(2)}) async-start(bf16[4,3,64,1792]{3,2,1,0:T(8,128)(2,1)} %bitcast.5), calls=%async_computation.2 | async-start | bytes 5505024 | tf_op jit(solution)/shard_map/all_to_all | solution.py:56
  49.8 166.5 %all-reduce.3.cloned.1.call-start = ((), (), s32[]{:S(2)}) async-start(), calls=%async_computation.11 | async-start | bytes 196608 | tf_op jit(solution)/shard_map/psum | solution.py:13
  51.9 52.1 %copy-start.4 = (bf16[3,64,1024]{2,1,0:T(8,128)(2,1)}, bf16[3,64,1024]{2,1,0:T(8,128)(2,1)S(1)}, u32[]{:S(2)}) copy-start(bf16[3,64,1024]{2,1,0:T(8,128)(2,1)S(1)} %gather_fusion.1) | copy-start | bytes 1179652
  103.9 61.7 %copy-start.11 = (s32[3]{0:T(128)S(1)}, s32[3]{0:T(128)}, u32[]{:S(2)}) copy-start(s32[3]{0:T(128)} %param.16) | copy-start | bytes 40
  165.6 218.5 %reduce-scatter.5.cloned.1.call-start = ((), (), s32[]{:S(2)}) async-start(), calls=%async_computation.10 | async-start | bytes 7077888 | tf_op jit(solution)/shard_map/reduce_scatter | solution.py:17
  281.3 142.5 %reduce-scatter.3.cloned.1.call-start = ((), (), s32[]{:S(2)}) async-start(), calls=%async_computation.8 | async-start | bytes 7077888 | tf_op jit(solution)/shard_map/reduce_scatter | solution.py:17
  311.9 0.7 copy-start.13
  311.9 1.2 copy-start.3
  311.9 1.2 copy-start.7
  313.3 5.9 %copy-start.8 = (bf16[3,128,64]{1,2,0:T(8,128)(2,1)S(1)}, bf16[3,128,64]{1,2,0:T(8,128)(2,1)}, u32[]{:S(2)}) copy-start(bf16[3,128,64]{1,2,0:T(8,128)(2,1)} %get-tuple-element.24) | copy-start | bytes 147460
  314.9 23.3 %all-to-all-start.3 = ((bf16[4,3,64,1024]{3,2,1,0:T(8,128)(2,1)}), bf16[4,3,64,1024]{3,2,1,0:T(8,128)(2,1)}, u32[]{:S(2)}, u32[]{:S(2)}) async-start(bf16[4,3,64,1024]{3,2,1,0:T(8,128)(2,1)} %select_convert_fusion.1), calls=%async_computation.5 | async-start | bytes 3145728 | tf_op jit(solution)/shard_map/all_to_all | solution.py:137
  321.7 21.1 %copy-start.10 = (s32[4,1,3]{2,1,0:T(1,128)S(1)}, s32[4,1,3]{2,1,0:T(1,128)}, u32[]{:S(2)}) copy-start(s32[4,1,3]{2,1,0:T(1,128)} %copy-done.9) | copy-start | bytes 148
  321.7 21.2 %copy-start.5 = (bf16[3,64,1024]{2,1,0:T(8,128)(2,1)S(1)}, bf16[3,64,1024]{2,1,0:T(8,128)(2,1)}, u32[]{:S(2)}) copy-start(bf16[3,64,1024]{2,1,0:T(8,128)(2,1)} %copy-done.4) | copy-start | bytes 1179652
  338.2 36.0 %all-to-all-start.4 = ((bf16[4,3,64,1792]{3,2,1,0:T(8,128)(2,1)}), bf16[4,3,64,1792]{3,2,1,0:T(8,128)(2,1)}, u32[]{:S(2)}, u32[]{:S(2)}) async-start(bf16[4,3,64,1792]{3,2,1,0:T(8,128)(2,1)} %select_convert_fusion), calls=%async_computation.6 | async-start | bytes 5505024 | tf_op jit(solution)/shard_map/all_to_all | solution.py:140
  381.2 42.6 %copy-start.1 = (bf16[16,64,1024]{2,1,0:T(8,128)(2,1)S(1)}, bf16[16,64,1024]{2,1,0:T(8,128)(2,1)}, u32[]{:S(2)}) copy-start(bf16[16,64,1024]{2,1,0:T(8,128)(2,1)} %param.18) | copy-start | bytes 6291460
Sparse Core Ops, SparseCore 0:
  9.6 67.4 all-gather.2
  78.7 63.3 all-gather.4
  165.7 50.5 all-reduce.2
  281.4 71.2 reduce-scatter.4
  355.6 68.1 reduce-scatter.2
where the time goes:
time: 439 us; the launch traced here: 431 us
  waiting for transfers between devices  210 us (48%)
  matrix products  153 us (35%)
  local copies, waits for them, and re-layouts  19.6 us (4%)
  starting transfers between devices  17.5 us (4%)
  between operations  14.2 us (3%)
  blocking collectives  9.6 us (2%)
  other arithmetic  7.42 us (2%)
    psum x1, waiting for transfers between devices, tensor_total(): return lax.psum(value.astype(jnp.bfloat16), 'tensor').astype(jnp.float32)  50.6 us
    all_gather x1, waiting for transfers between devices, body(): lax.all_gather(cotangent, 'tensor', axis=1, tiled=True)  38.2 us
    reduce_scatter x2, waiting for transfers between devices, common_result(): lax.psum_scatter(value.astype(jnp.bfloat16), 'tensor', scatter_dimension=...  37 us
    dot_general x1, matrix products, body(): jnp.dot(hidden, down_weight, preferred_element_type=jnp.float32)  30.5 us
    all_to_all x1, waiting for transfers between devices, body(): lax.all_to_all(up_b[safe], 'dp', split_axis=0, concat_axis=0, tiled=True)  28.4 us
    all_to_all x1, waiting for transfers between devices, body(): lax.all_to_all(outgoing_out.astype(jnp.bfloat16), 'dp', split_axis=0, con...  23.8 us
    dot_general x1, matrix products, body(): lax.dot_general(d_gate, gate_weight, contract, preferred_element_type=jnp...  22.7 us
    dot_general x1, matrix products, body(): lax.dot_general(lax.all_gather(cotangent, 'tensor', axis=1, tiled=True),...  22.2 us
  transfers between devices with their start and end apart: 9, of which 7 were waited for; matrix products, arithmetic and copies ran while one was open for 20% of the time, Pallas kernels for 0%

commit v1 on v0

v1 whole, which is shorter than its diff:
```python
import functools

import jax
import jax.numpy as jnp
from jax import lax
from jax.experimental import pallas as pl
from jax.experimental.pallas import tpu as pltpu
from jax.sharding import PartitionSpec as P

BLOCK = 128
adapter_scale = 0.25
VMEM_LIMIT = 32 * 1024 * 1024
COVER = 1 << 32
f32 = jnp.float32
bf16 = jnp.bfloat16
NT = (((1,), (1,)), ((), ()))


def params():
    return pltpu.CompilerParams(vmem_limit_bytes=VMEM_LIMIT)


def tile_of(size, most=256):
    return next((t for t in range(most, 127, -128) if size % t == 0), size)


def ordered_call(kernel, *, grid, in_specs, out_specs, out_shape, name, flops=1 << 27, prefetch=0, scratch=(), after=()):
    many = prefetch + len(in_specs)
    outs = len(out_specs)

    def run(*refs):
        mark = refs[many + len(after) + outs]
        mark[...] = jnp.zeros_like(mark)
        kernel(*refs[:many], *refs[many + len(after) : many + len(after) + outs], *refs[many + len(after) + outs + 1 :])

    call = pl.pallas_call(
        run,
        grid_spec=pltpu.PrefetchScalarGridSpec(
            num_scalar_prefetch=prefetch,
            grid=grid,
            in_specs=list(in_specs) + [pl.BlockSpec(memory_space=pl.ANY)] * len(after),
            out_specs=list(out_specs) + [pl.BlockSpec((8, 128), lambda *_: (0, 0))],
            scratch_shapes=list(scratch),
        ),
        out_shape=list(out_shape) + [jax.ShapeDtypeStruct((8, 128), f32)],
        compiler_params=params(),
        cost_estimate=pl.CostEstimate(flops=flops, bytes_accessed=flops // 384, transcendentals=0),
        name=name,
    )
    return lambda *operands: call(*operands, *after)


def adapter_rows(count):
    return [slice(i * BLOCK, (i + 1) * BLOCK) for i in range(count)]


def forward_part(ids, shards, gate_weight, up_weight, sums, after):
    rows, width = shards[0].shape
    hidden = gate_weight.shape[1]
    tile = tile_of(hidden)
    many = len(shards)

    def kernel(ids_ref, *refs):
        xs, gs, us = refs[:many], refs[many : 2 * many], refs[2 * many : 3 * many]
        g = u = None
        if sums:
            g, u = refs[3 * many][...], refs[3 * many + 1][...]
        for x, wg, wu in zip(xs, gs, us):
            a = x[...]
            pg = jnp.dot(a, wg[...], preferred_element_type=f32)
            pu = jnp.dot(a, wu[...], preferred_element_type=f32)
            g, u = (pg, pu) if g is None else (g + pg, u + pu)
        refs[-2][...] = g
        refs[-1][...] = u

    whole = pl.BlockSpec((rows, width), lambda t, ids: (0, 0))
    weights = [pl.BlockSpec((width, tile), lambda t, ids, i=i: (ids[i], t)) for i in range(many)]
    acc = pl.BlockSpec((rows, tile), lambda t, ids: (0, t))
    shape = jax.ShapeDtypeStruct((rows, hidden), f32)
    return ordered_call(
        kernel,
        prefetch=1,
        grid=(hidden // tile,),
        in_specs=[whole] * many + weights + weights + [acc] * len(sums),
        out_specs=[acc, acc],
        out_shape=[shape, shape],
        name="forward_part",
        flops=4 * many * rows * width * hidden,
        after=after,
    )(ids, *shards, *[gate_weight] * many, *[up_weight] * many, *sums)


def activate(gate, up, low_b, factor, after):
    rows, hidden = gate.shape
    tile = tile_of(hidden, 512)
    count, rank = factor.shape[0], factor.shape[1]

    def kernel(g_ref, u_ref, low_ref, b_ref, h_ref, act_ref, slope_ref):
        for i, part in enumerate(adapter_rows(count)):
            g = g_ref[part]
            u = u_ref[part] + adapter_scale * jnp.dot(low_ref[part], b_ref[i], preferred_element_type=f32)
            s = jax.nn.sigmoid(g)
            act = g * s
            act_ref[part] = act
            h_ref[part] = (act * u).astype(bf16)
            slope_ref[part] = u * s * (1.0 + g * (1.0 - s))

    acc = pl.BlockSpec((rows, tile), lambda t: (0, t))
    return ordered_call(
        kernel,
        grid=(hidden // tile,),
        in_specs=[
            acc, acc,
            pl.BlockSpec((rows, rank), lambda t: (0, 0)),
            pl.BlockSpec((count, rank, tile), lambda t: (0, 0, t)),
        ],
        out_specs=[acc, acc, acc],
        out_shape=[
            jax.ShapeDtypeStruct((rows, hidden), bf16),
            jax.ShapeDtypeStruct((rows, hidden), f32),
            jax.ShapeDtypeStruct((rows, hidden), f32),
        ],
        name="activate",
        flops=1 << 31,
        after=after,
    )(gate, up, low_b, factor)


def hidden_product(x_refs, w_refs):
    return functools.reduce(
        jnp.add,
        [lax.dot_general(x[...], w[...], NT, preferred_element_type=f32) for x, w in zip(x_refs, w_refs)],
    )


def hidden_part(ids, shards, down_weight, after):
    rows, width = shards[0].shape
    hidden = down_weight.shape[0]
    tile = tile_of(hidden)
    many = len(shards)

    def kernel(ids_ref, *refs):
        refs[-1][...] = hidden_product(refs[:many], refs[many:-1])

    whole = pl.BlockSpec((rows, width), lambda t, ids: (0, 0))
    weights = [pl.BlockSpec((tile, width), lambda t, ids, i=i: (t, ids[i])) for i in range(many)]
    return ordered_call(
        kernel,
        prefetch=1,
        grid=(hidden // tile,),
        in_specs=[whole] * many + weights,
        out_specs=[pl.BlockSpec((rows, tile), lambda t, ids: (0, t))],
        out_shape=[jax.ShapeDtypeStruct((rows, hidden), f32)],
        name="hidden_part",
        flops=2 * many * rows * width * hidden,
        after=after,
    )(ids, *shards, *([down_weight] * many))


def hidden_gradients(ids, shards, down_weight, total, act, slope, low_b, factor, after):
    rows, width = shards[0].shape
    hidden = down_weight.shape[0]
    tile = tile_of(hidden)
    count, rank = factor.shape[0], factor.shape[1]
    many = len(shards)

    def kernel(ids_ref, *refs):
        d_ref, act_ref, slope_ref, low_ref, b_ref, dg_ref, du_ref, dl_ref, gb_ref = refs[2 * many :]
        d = d_ref[...] + hidden_product(refs[:many], refs[many : 2 * many])
        dg_ref[...] = (d * slope_ref[...]).astype(bf16)
        du = (d * act_ref[...]).astype(bf16)
        du_ref[...] = du

        @pl.when(pl.program_id(0) == 0)
        def _():
            dl_ref[...] = jnp.zeros_like(dl_ref)

        for i, part in enumerate(adapter_rows(count)):
            dl_ref[part] += lax.dot_general(du[part], b_ref[i], NT, preferred_element_type=f32)
            grad = lax.dot_general(low_ref[part], du[part], (((0,), (0,)), ((), ())), preferred_element_type=f32)
            gb_ref[i] = (adapter_scale * grad).astype(bf16)

    whole = pl.BlockSpec((rows, width), lambda t, ids: (0, 0))
    weights = [pl.BlockSpec((tile, width), lambda t, ids, i=i: (t, ids[i])) for i in range(many)]
    acc = pl.BlockSpec((rows, tile), lambda t, ids: (0, t))
    lows = pl.BlockSpec((rows, rank), lambda t, ids: (0, 0))
    factors = pl.BlockSpec((count, rank, tile), lambda t, ids: (0, 0, t))
    return ordered_call(
        kernel,
        prefetch=1,
        grid=(hidden // tile,),
        in_specs=[whole] * many + weights + [acc, acc, acc, lows, factors],
        out_specs=[acc, acc, lows, factors],
        out_shape=[
            jax.ShapeDtypeStruct((rows, hidden), bf16),
            jax.ShapeDtypeStruct((rows, hidden), bf16),
            jax.ShapeDtypeStruct((rows, rank), f32),
            jax.ShapeDtypeStruct((count, rank, hidden), bf16),
        ],
        name="hidden_gradients",
        flops=2 * many * rows * width * hidden,
        after=after,
    )(ids, *shards, *([down_weight] * many), total, act, slope, low_b, factor)


def mixed_parts(ids, x, down_weight, width, after):
    rows, hidden = x.shape
    tile = tile_of(width, 512)
    steps = width // tile
    pairs = ids.shape[0] // 2

    def kernel(ids_ref, x_ref, wa, wb, oa, ob):
        oa[0] = jnp.dot(x_ref[...], wa[...], preferred_element_type=f32).astype(bf16)
        ob[0] = jnp.dot(x_ref[...], wb[...], preferred_element_type=f32).astype(bf16)

    out = pl.BlockSpec((1, rows, tile), lambda j, t, ids: (j, 0, t))
    shape = jax.ShapeDtypeStruct((pairs, rows, width), bf16)
    return ordered_call(
        kernel,
        prefetch=1,
        grid=(pairs, steps),
        in_specs=[
            pl.BlockSpec((rows, hidden), lambda j, t, ids: (0, 0)),
            pl.BlockSpec((hidden, tile), lambda j, t, ids: (0, ids[2 * j] * steps + t)),
            pl.BlockSpec((hidden, tile), lambda j, t, ids: (0, ids[2 * j + 1] * steps + t)),
        ],
        out_specs=[out, out],
        out_shape=[shape, shape],
        name="mixed_parts",
        flops=4 * pairs * rows * width * hidden,
        after=after,
    )(ids, x, down_weight, down_weight)


def item_part(ids, d_gate, d_up, gate_weight, up_weight, width, after):
    rows, hidden = d_gate.shape
    shards = ids.shape[0]
    tile = tile_of(width, 512)
    steps = width // tile

    def kernel(ids_ref, dg, du, *refs):
        for i in range(shards):
            total = lax.dot_general(dg[...], refs[2 * i][...], NT, preferred_element_type=f32)
            total = total + lax.dot_general(du[...], refs[2 * i + 1][...], NT, preferred_element_type=f32)
            refs[2 * shards + i][0] = total.astype(bf16)

    whole = pl.BlockSpec((rows, hidden), lambda t, ids: (0, 0))
    specs = [whole, whole]
    for i in range(shards):
        specs += [pl.BlockSpec((tile, hidden), lambda t, ids, i=i: (ids[i] * steps + t, 0))] * 2
    return ordered_call(
        kernel,
        prefetch=1,
        grid=(steps,),
        in_specs=specs,
        out_specs=[pl.BlockSpec((1, rows, tile), lambda t, ids: (0, 0, t))] * shards,
        out_shape=[jax.ShapeDtypeStruct((1, rows, width), bf16)] * shards,
        name="item_part",
        flops=4 * shards * rows * width * hidden,
        after=after,
    )(ids, d_gate, d_up, *([gate_weight, up_weight] * shards))


def copy_chosen(index, options, after):
    rows, width = options[0].shape
    half = rows // 2

    def kernel(index_ref, *refs):
        for i in range(len(options)):

            @pl.when(index_ref[0] == i)
            def _():
                refs[-1][...] = refs[i][...]

    def block(i):
        return pl.BlockSpec((half, width), lambda t, index: (jnp.where(index[0] == i, t, 0), 0))

    return ordered_call(
        kernel,
        prefetch=1,
        grid=(2,),
        in_specs=[block(i) for i in range(len(options))],
        out_specs=[pl.BlockSpec((half, width), lambda t, index: (t, 0))],
        out_shape=[jax.ShapeDtypeStruct((rows, width), bf16)],
        name="copy_chosen",
        after=after,
    )(index, *options)


def copy_both(arrays, after):
    rows, width = arrays[0].shape
    many = len(arrays)

    def kernel(*refs):
        for i in range(many):
            refs[many + i][...] = refs[i][...]

    block = pl.BlockSpec((rows // 2, width), lambda t: (t, 0))
    return ordered_call(
        kernel,
        grid=(2,),
        in_specs=[block] * many,
        out_specs=[block] * many,
        out_shape=[jax.ShapeDtypeStruct(x.shape, x.dtype) for x in arrays],
        name="copy_both",
        after=after,
    )(*arrays)


def copy_small(arrays, after):
    many = len(arrays)

    def kernel(*refs):
        for i in range(many):
            refs[many + i][...] = refs[i][...]

    block = pl.BlockSpec(arrays[0].shape, lambda t: (0,) * arrays[0].ndim)
    return ordered_call(
        kernel,
        grid=(1,),
        in_specs=[block] * many,
        out_specs=[block] * many,
        out_shape=[jax.ShapeDtypeStruct(x.shape, x.dtype) for x in arrays],
        name="copy_small",
        after=after,
    )(*arrays)


def line_sums(wanted, parts, received, extra, after, flops=1 << 27):
    rows, width = parts[0][0].shape[1:]
    half = rows // 2
    outs = len(received)
    arrays = [x for pair in parts for x in pair]
    others = [x for group in received for x in group] + extra

    def kernel(wanted_ref, *refs):
        step = 0
        ins = refs[: outs * len(arrays)]
        adds = list(refs[outs * len(arrays) : -outs])
        for k in range(outs):
            terms = [adds.pop(0)[...].astype(f32) for _ in received[k]]
            terms += [x[...] for x in adds[len(adds) - len(extra) :]] if k == outs - 1 else []

            for i in range(len(parts)):

                @pl.when(wanted_ref[2 * k] == i)
                def _():
                    mine, theirs = ins[step + 2 * i], ins[step + 2 * i + 1]
                    total = functools.reduce(jnp.add, terms, mine[0].astype(f32) + theirs[0].astype(f32))
                    refs[len(refs) - outs + k][...] = total.astype(bf16)

            step += len(arrays)

    def block(k, i):
        def where(t, wanted):
            hit = wanted[2 * k] == i // 2
            return (jnp.where(hit, wanted[2 * k + 1], 0), jnp.where(hit, t, 0), 0)

        return pl.BlockSpec((1, half, width), where)

    flat = pl.BlockSpec((half, width), lambda t, wanted: (t, 0))
    return ordered_call(
        kernel,
        prefetch=1,
        grid=(2,),
        in_specs=[block(k, i) for k in range(outs) for i in range(len(arrays))] + [flat] * len(others),
        out_specs=[flat] * outs,
        out_shape=[jax.ShapeDtypeStruct((rows, width), bf16)] * outs,
        name="line_sums",
        flops=flops,
        after=after,
    )(wanted, *arrays * outs, *others)


def sum_small(arrays, after):
    def kernel(*refs):
        refs[-1][...] = functools.reduce(jnp.add, [x[...] for x in refs[:-1]])

    block = pl.BlockSpec(arrays[0].shape, lambda t: (0, 0))
    return ordered_call(
        kernel,
        grid=(1,),
        in_specs=[block] * len(arrays),
        out_specs=[block],
        out_shape=[jax.ShapeDtypeStruct(arrays[0].shape, f32)],
        name="sum_small",
        after=after,
    )(*arrays)


def low_rank(tokens, factor, after):
    rows, width = tokens.shape
    count, rank = factor.shape[:2]

    def kernel(x_ref, a_ref, o_ref):
        for i, part in enumerate(adapter_rows(count)):
            o_ref[part] = lax.dot_general(x_ref[part], a_ref[i], NT, preferred_element_type=f32)

    return ordered_call(
        kernel,
        grid=(1,),
        in_specs=[
            pl.BlockSpec((rows, width), lambda t: (0, 0)),
            pl.BlockSpec(factor.shape, lambda t: (0, 0, 0)),
        ],
        out_specs=[pl.BlockSpec((rows, rank), lambda t: (0, 0))],
        out_shape=[jax.ShapeDtypeStruct((rows, rank), f32)],
        name="low_rank",
        after=after,
    )(tokens, factor)


def low_rank_gradients(fill, lows, tokens, factor, after):
    rows, width = tokens.shape
    count, rank = factor.shape[:2]

    def kernel(fill_ref, x_ref, a_ref, *refs):
        d_low = functools.reduce(jnp.add, [x[...] for x in refs[:-2]])
        for i, part in enumerate(adapter_rows(count)):
            alive = lax.broadcasted_iota(jnp.int32, (BLOCK, rank), 0) < fill_ref[i]
            d = jnp.where(alive, adapter_scale * d_low[part], 0.0).astype(bf16)
            grad = lax.dot_general(d, x_ref[part], (((0,), (0,)), ((), ())), preferred_element_type=f32)
            refs[-2][i] = grad.astype(bf16)
            refs[-1][part] = jnp.dot(d, a_ref[i], preferred_element_type=f32)

    block = pl.BlockSpec(factor.shape, lambda t, fill: (0, 0, 0))
    whole = pl.BlockSpec((rows, width), lambda t, fill: (0, 0))
    return ordered_call(
        kernel,
        prefetch=1,
        grid=(1,),
        in_specs=[whole, block] + [pl.BlockSpec((rows, rank), lambda t, fill: (0, 0))] * len(lows),
        out_specs=[block, whole],
        out_shape=[jax.ShapeDtypeStruct(factor.shape, bf16), jax.ShapeDtypeStruct((rows, width), f32)],
        name="low_rank_gradients",
        flops=COVER,
        after=after,
    )(fill, tokens, factor, *lows)


def pick_slots(places, in_factor, out_factor, after):
    many = places.shape[0]

    def kernel(places_ref, a_ref, b_ref, oa, ob):
        held = places_ref[pl.program_id(0)] >= 0

        @pl.when(held)
        def _():
            oa[...] = a_ref[...]
            ob[...] = b_ref[...]

        @pl.when(~held)
        def _():
            oa[...] = jnp.zeros_like(oa)
            ob[...] = jnp.zeros_like(ob)

    def block(factor):
        return (1,) + factor.shape[1:]

    picked = [pl.BlockSpec(block(f), lambda i, ids: (jnp.maximum(ids[i], 0), 0, 0)) for f in (in_factor, out_factor)]
    out = [pl.BlockSpec(block(f), lambda i, ids: (i, 0, 0)) for f in (in_factor, out_factor)]
    return ordered_call(
        kernel,
        prefetch=1,
        grid=(many,),
        in_specs=picked,
        out_specs=out,
        out_shape=[jax.ShapeDtypeStruct((many,) + f.shape[1:], bf16) for f in (in_factor, out_factor)],
        name="pick_slots",
        after=after,
    )(places, in_factor, out_factor)


def slot_sums(places, grads, slots, after, flops=1 << 27):
    total_blocks, rank, width = grads.shape

    def kernel(places_ref, *rest):
        ins, out, total = rest
        out[...] = jnp.zeros_like(out)
        for i in range(total_blocks):
            place = places_ref[i]
            earlier = functools.reduce(jnp.logical_or, [places_ref[j] == place for j in range(i)], False)
            later = functools.reduce(jnp.logical_or, [places_ref[j] == place for j in range(i + 1, total_blocks)], False)
            here = ins.at[i]
            held = place >= 0

            @pl.when(held & ~jnp.logical_or(earlier, later))
            def _():
                out[pl.ds(jnp.maximum(place, 0), 1)] = here[...][None]

            @pl.when(held & ~jnp.asarray(earlier) & later)
            def _():
                total[...] = here[...].astype(f32)
                for j in range(i + 1, total_blocks):

                    @pl.when(places_ref[j] == place)
                    def _():
                        total[...] += ins[j].astype(f32)

                out[pl.ds(jnp.maximum(place, 0), 1)] = total[...].astype(bf16)[None]

    return ordered_call(
        kernel,
        prefetch=1,
        grid=(1,),
        in_specs=[pl.BlockSpec((total_blocks, rank, width), lambda s, ids: (0, 0, 0))],
        out_specs=[pl.BlockSpec((slots, rank, width), lambda s, ids: (0, 0, 0))],
        scratch=[pltpu.VMEM((rank, width), f32)],
        out_shape=[jax.ShapeDtypeStruct((slots, rank, width), bf16)],
        name="slot_sums",
        flops=flops,
        after=after,
    )(places, grads)


def line_pairs(sources, step):
    return [(2 * z + core, 2 * (z + step) + core) for z in sources for core in (0, 1)]


def swap_cores(x, chips):
    return lax.ppermute(x, "tensor", [(i, i ^ 1) for i in range(2 * chips)])


def arrival_order(chips):
    order = []
    for z in range(chips):
        up, down = list(range(z + 1, chips)), list(range(z - 1, -1, -1))
        order.append([z] + (up + down if 2 * z < chips else down + up))
    return order


def line_hop(left, right, s, chips):
    return [
        lax.ppermute(left, "tensor", line_pairs(range(s - 1, chips - 1), 1)),
        lax.ppermute(right, "tensor", line_pairs(range(1, chips - s + 1), -1)),
    ]


def last_hop(shard, chips):
    both = lax.ppermute(shard, "tensor", line_pairs([chips - 2], 1) + line_pairs([1], -1))
    return [both, both]


def stage_shard(chip, left, right, j, chips, after):
    options, where = [], []
    for z, row in enumerate(arrival_order(chips)):
        value = left[z - row[j]] if row[j] <= z else right[row[j] - z]
        spot = next((i for i, option in enumerate(options) if option is value), len(options))
        if spot == len(options):
            options.append(value)
        where.append(spot)
    return copy_chosen(jnp.array(where, jnp.int32)[chip][None], options, after)


def send_order(chips):
    order = []
    for z in range(chips):
        due = []
        for s in range(1, chips):
            if z <= s - 1:
                due.append(chips - s + z)
            if z >= chips - s:
                due.append(s - chips + z)
        order.append(due + [z])
    return order


def scatter_sums(chip, parts, received, s, chips, after):
    stage = [{d: j for j, d in enumerate(row)} for row in send_order(chips)]
    entries = [(i, k) for i, pair in enumerate(parts) for k in range(pair[0].shape[0])]

    def named(table):
        return jnp.array(table, jnp.int32)[chip]

    if s == 1:
        wanted = named([entries[0]] * chips)
        return line_sums(wanted, parts[:1], [[]], [], after)
    up = [entries[stage[z][chips - s + z]] if z <= s - 1 else entries[0] for z in range(chips)]
    down = [entries[stage[z][s - chips + z]] if z >= chips - s else entries[0] for z in range(chips)]
    wanted = named([list(a) + list(b) for a, b in zip(up, down)])
    return line_sums(wanted, parts, [[received[0]], [received[1]]], [], after)


def scatter_hop(payload, s, chips):
    up, down = line_pairs(range(0, s), 1), line_pairs(range(chips - s, chips), -1)
    if len(payload) == 1:
        both = lax.ppermute(payload[0], "tensor", up + down)
        return [both, both]
    return [lax.ppermute(payload[0], "tensor", up), lax.ppermute(payload[1], "tensor", down)]


def scatter_end(part, received, extra, after):
    entry = part[0].shape[0] - 1
    return line_sums(jnp.array([0, entry], jnp.int32), [part], [list(received)], extra, after)


def body(
    tokens,
    cotangent,
    gate_weight,
    up_weight,
    down_weight,
    block_task,
    block_fill,
    task_slot,
    inner_correction_weights,
    up_b,
):
    size, groups = lax.axis_size("tensor"), lax.axis_size("dp")
    chips = size // 2
    last, half = chips - 1, chips // 2
    me, group = lax.axis_index("tensor"), lax.axis_index("dp")
    chip, core = me // 2, me % 2
    rows, width = tokens.shape
    count = block_task.shape[0]
    slots, rank = inner_correction_weights.shape[:2]
    distances = [1 << i for i in range(size.bit_length() - 1)]

    def exchange(x, r):
        return lax.ppermute(x, "dp", [(d, d ^ r) for d in range(groups)])

    def from_distance(x, distance):
        return lax.ppermute(x, "tensor", [(i, i ^ distance) for i in range(size)])

    def pairs(table):
        return jnp.stack([2 * table + core, 2 * table + 1 - core], axis=1).reshape(-1).astype(jnp.int32)

    order = pairs(jnp.array(arrival_order(chips), jnp.int32)[chip])
    targets = pairs(jnp.array(send_order(chips), jnp.int32)[chip])

    hop = line_hop(tokens, tokens, 1, chips)
    shards = [tokens, swap_cores(tokens, chips)]
    task_ids = jnp.arange(task_slot.shape[0], dtype=jnp.int32)
    slot = jnp.sum(jnp.where(block_task[:, None] == task_ids[None, :], task_slot[None, :], 0), axis=1)
    wanted, bit = slot, 1
    while bit < groups:
        theirs = exchange(wanted, bit)
        low_side = (group & bit) == 0
        wanted = jnp.concatenate([jnp.where(low_side, wanted, theirs), jnp.where(low_side, theirs, wanted)])
        bit *= 2
    place = wanted - group * slots
    places = jnp.where(jnp.logical_and(place >= 0, place < slots), place, -1)

    left, right, sums, mark = [tokens], [tokens], [], None
    begun = 0
    for j in range(1, chips):
        left.append(hop[0])
        right.append(hop[1])
        if j < last - 1:
            hop = line_hop(left[j], right[j], j + 1, chips)
        mine, mark = stage_shard(chip, left, right, j, chips, [mark] if j > 1 else [])
        if j == 1:
            picked_in, picked_out, mark = pick_slots(places, inner_correction_weights, up_b, [mark])
            factor_in = lax.psum_scatter(picked_in, "dp", scatter_dimension=0, tiled=True)
            factor_out = lax.psum_scatter(picked_out, "dp", scatter_dimension=0, tiled=True)
        if j == last - 1:
            hop = last_hop(mine, chips)
        shards += [mine, swap_cores(mine, chips)]
        if j in (half - 1, last - 1):
            *sums, mark = forward_part(
                order[2 * begun : 2 * j + 2], shards, gate_weight, up_weight, sums, [mark]
            )
            shards, begun = [], j + 1
        if j == last - 1:
            low, mark = low_rank(tokens, factor_in, [mark])
            low, mark = sum_small([low, from_distance(low, 1)], [mark])
            cotangent, mark = copy_both([cotangent], [mark])
    far = [from_distance(low, 2 * k) for k in range(1, chips)]
    cotangent_hop = line_hop(cotangent, cotangent, 1, chips)
    cotangent_other = swap_cores(cotangent, chips)
    gate, up, mark = forward_part(order[2 * begun :], shards, gate_weight, up_weight, sums, [mark])
    low = sum_small([low] + far, [mark])[0]
    live = (jnp.arange(BLOCK, dtype=jnp.int32)[None, :] < block_fill[:, None]).astype(f32)[..., None]
    low_b = (low.reshape(count, BLOCK, rank) * live).astype(bf16).reshape(rows, rank)
    left, right = [cotangent], [cotangent]
    hidden_b, act, slope, mark = activate(gate, up, low_b, factor_out, [mark])
    first = copy_both(cotangent_hop, [mark])
    left.append(first[0])
    right.append(first[1])
    cotangent_hop = line_hop(left[1], right[1], 2, chips)

    def mixed_part(which, after):
        mine, theirs, mark = mixed_parts(targets[which], hidden_b, down_weight, width, after)
        return (mine, swap_cores(theirs, chips)), mark

    mixed = []
    part, mark = mixed_part(slice(0, 2), [first[-1]])
    mixed.append(part)
    part, mark = mixed_part(slice(2, 2 * chips), [mark])
    mixed.append(part)
    shards = [cotangent, cotangent_other]
    for j in range(1, chips):
        if j > 1:
            left.append(cotangent_hop[0])
            right.append(cotangent_hop[1])
            if j < last - 1:
                cotangent_hop = line_hop(left[j], right[j], j + 1, chips)
        value, mark = stage_shard(chip, left, right, j, chips, [mark])
        if j == last - 1:
            cotangent_hop = last_hop(value, chips)
            *payload, mark = scatter_sums(chip, mixed, None, 1, chips, [mark])
            mixed_hop = scatter_hop(payload, 1, chips)
            total, mark = hidden_part(order[: 2 * half], shards[: 2 * half], down_weight, [mark])
        shards += [value, swap_cores(value, chips)]
    *payload, mark = scatter_sums(chip, mixed, mixed_hop, 2, chips, [mark])
    mixed_hop = scatter_hop(payload, 2, chips)
    d_gate, d_up, d_low, out_grad, mark = hidden_gradients(
        order[2 * half :], shards[2 * half :], down_weight, total, act, slope, low_b, factor_out, [mark]
    )

    def item(which, after):
        return item_part(targets[which], d_gate, d_up, gate_weight, up_weight, width, after)

    out_grads = lax.all_gather(out_grad, "dp", axis=0, tiled=True)
    near_low = from_distance(d_low, distances[0])
    for s in range(3, chips):
        *payload, mark = scatter_sums(chip, mixed, mixed_hop, s, chips, [mark])
        mixed_hop = scatter_hop(payload, s, chips)
    theirs, mark = item(slice(1, 2), [mark])
    theirs = swap_cores(theirs, chips)
    d_low, mark = sum_small([d_low, near_low], [mark])
    far_low = from_distance(d_low, distances[1])
    mine, mark = item(slice(0, 1), [mark])
    parts = [(mine, theirs)]
    for distance in distances[2:]:
        d_low, mark = sum_small([d_low, far_low], [mark])
        far_low = from_distance(d_low, distance)
    item_hop = None
    bits = [1 << i for i in range(groups.bit_length() - 1)]
    for j in range(1, chips):
        *payload, mark = scatter_sums(chip, parts, item_hop, j, chips, [mark])
        item_hop = scatter_hop(payload, j, chips)
        mine, theirs, mark = item(slice(2 * j, 2 * j + 2), [mark])
        parts.append((mine, swap_cores(theirs, chips)))
        if j == 1:
            in_grad, through, mark = low_rank_gradients(
                block_fill, [d_low, far_low], tokens, factor_in, [mark]
            )
            in_grads = {0: in_grad} | {bit: exchange(in_grad, bit) for bit in bits}
            mixed, mark = scatter_end(mixed[-1], mixed_hop, [], [mark])
        if j == 2:
            out_sums, mark = slot_sums(places, out_grads, slots, [mark])
            near = copy_small([in_grads[bit] for bit in bits], [mark])
            mark = near[-1]
            in_grads |= dict(zip(bits, near))
            for r in range(1, groups):
                if r not in in_grads:
                    top = 1 << (r.bit_length() - 1)
                    in_grads[r] = exchange(in_grads[top], r ^ top)
    near_places = jnp.concatenate(
        [lax.dynamic_slice_in_dim(places, (group ^ r) * count, count, 0) for r in range(groups)]
    )
    in_grads = jnp.concatenate([in_grads[r] for r in range(groups)])
    in_sums, mark = slot_sums(near_places, in_grads, slots, [mark], flops=COVER)
    item_derivative = scatter_end(parts[-1], item_hop, [through], [mark])[0]
    return (mixed, item_derivative, in_sums, out_sums)


def solution(mesh):
    return jax.shard_map(
        body,
        mesh=mesh,
        in_specs=(
            P("dp", "tensor"),
            P("dp", "tensor"),
            P(None, "tensor"),
            P(None, "tensor"),
            P("tensor", None),
            P("dp"),
            P("dp"),
            P(),
            P("dp", None, "tensor"),
            P("dp", None, "tensor"),
        ),
        out_specs=(
            P("dp", "tensor"),
            P("dp", "tensor"),
            P("dp", None, "tensor"),
            P("dp", None, "tensor"),
        ),
        check_vma=False,
    )
```

time: 439 us -> 377 us (0.86); the launches traced: 431 us -> 375 us
  Pallas kernels: 0 us -> 172 us
  matrix products: 153 us -> 0 us
  waiting for transfers between devices: 210 us -> 63.4 us
  starting transfers between devices: 17.5 us -> 76.5 us
  local copies, waits for them, and re-layouts: 19.6 us -> 44 us
  blocking collectives: 9.6 us -> 0 us
    pallas_call x0 -> x39, Pallas kernels: none -> 172 us  [ordered_call(): return lambda *operands: call(*operands, *after)]
    dot_general x14 -> x0, matrix products: 153 us -> none  [the longest x1 30.5 us: body(): jnp.dot(hidden, down_weight, preferred_element_type=jnp.float32)]
    all_to_all x4 -> x0, waiting for transfers between devices: 82.4 us -> none  [the longest x1 28.4 us: body(): lax.all_to_all(up_b[safe], 'dp', split_axis=0, concat_axis=0, tiled=True)]
    ppermute x0 -> x46, starting transfers between devices: none -> 76.4 us  [the longest x4 21.8 us: scatter_hop(): lax.ppermute(payload[0], 'tensor', up)]
    ppermute x0 -> x46, waiting for transfers between devices: none -> 62.7 us  [the longest x7 24.2 us: from_distance(): return lax.ppermute(x, 'tensor', [(i, i ^ distance) for i in range(size)])]
    psum x1 -> x0, waiting for transfers between devices: 50.6 us -> none  [tensor_total(): return lax.psum(value.astype(jnp.bfloat16), 'tensor').astype(jnp.float32)]
    all_gather x2 -> x1, waiting for transfers between devices: 38.2 us -> 0.01 us  [body(): out_grads = lax.all_gather(out_grad, 'dp', axis=0, tiled=True)]
    reduce_scatter x2 -> x0, waiting for transfers between devices: 37 us -> none  [common_result(): lax.psum_scatter(value.astype(jnp.bfloat16), 'tensor', scatter_dimension=...]
  transfers between devices with their start and end apart: 9 -> 49, of which waited for: 7 -> 16; matrix products, arithmetic and copies ran while one was open for 20% -> 3% of each run, Pallas kernels for 0% -> 44%
where the time goes in v1:
time: 377 us; the launch traced here: 375 us
  Pallas kernels  172 us (46%)
  starting transfers between devices  76.5 us (20%)
  waiting for transfers between devices  63.4 us (17%)
  local copies, waits for them, and re-layouts  44 us (12%)
  between operations  14.7 us (4%)
  other arithmetic  4.18 us (1%)
    pallas_call x39, Pallas kernels, ordered_call(): return lambda *operands: call(*operands, *after)  172 us
    unnamed x122, local copies, waits for them, and re-layouts  36.4 us
    ppermute x7, waiting for transfers between devices, from_distance(): return lax.ppermute(x, 'tensor', [(i, i ^ distance) for i in range(size)])  24.2 us
    ppermute x4, starting transfers between devices, scatter_hop(): lax.ppermute(payload[0], 'tensor', up)  21.8 us
    ppermute x2, starting transfers between devices, scatter_hop(): both = lax.ppermute(payload[0], 'tensor', up + down)  16.4 us
    ppermute x4, waiting for transfers between devices, scatter_hop(): lax.ppermute(payload[0], 'tensor', up)  12.5 us
    ppermute x4, starting transfers between devices, line_hop(): lax.ppermute(left, 'tensor', line_pairs(range(s - 1, chips - 1), 1))  9.68 us
    ppermute x4, waiting for transfers between devices, line_hop(): lax.ppermute(right, 'tensor', line_pairs(range(1, chips - s + 1), -1))  8.97 us
  transfers between devices with their start and end apart: 49, of which 16 were waited for; matrix products, arithmetic and copies ran while one was open for 3% of the time, Pallas kernels for 44%

profile of v1, /device:TPU:0, one launch (start us, length us, event | category | flops | bytes accessed | tf_op | source)
XLA Modules:
  0.0 375.0 jit_solution(17206858861625027902)
XLA Ops:
  8.5 5.6 %collective-permute-start.2 = (bf16[384,1024]{1,0:T(8,128)(2,1)}, bf16[384,1024]{1,0:T(8,128)(2,1)S(1)}, u32[]{:S(2)}, u32[]{:S(2)}) collective-permute-start(bf16[384,1024]{1,0:T(8,128)(2,1)} %refs_1_.5), channel_id=1, source_target_pairs={{0,2},{1,3},{2,4},{3,5},{4,6},{5,7},{8,10},{9,11},{10,12},{11,13},... | collective-permute-start | bytes 2359304 | tf_op jit(solution)/shard_map/ppermute | solution.py:534
  22.4 7.5 %collective-permute-done.refs_1_.refs_3_ = bf16[384,1024]{1,0:T(8,128)(2,1)S(1)} collective-permute-done((bf16[384,1024]{1,0:T(8,128)(2,1)}, bf16[384,1024]{1,0:T(8,128)(2,1)S(1)}, u32[]{:S(2)}, u32[]{:S(2)}) %collective-permute-start) | collective-permute-done | bytes 786464 | tf_op jit(solution)/shard_map/ppermute | solution.py:535
  45.2 18.5 %forward_part.3 = (f32[384,1792]{1,0:T(8,128)S(1)}, f32[384,1792]{1,0:T(8,128)S(1)}, f32[8,128]{1,0:T(8,128)S(1)}) custom-call(s32[4]{0:T(128)S(1)} %slice.66.refs_0_, bf16[384,1024]{1,0:T(8,128)(2,1)S(1)} %copy-done.18, bf16[384,1024]{1,0:T(8,128)(2,1)} %collective-permute-done.4.refs_2_, bf16[384,1024]{1,0:T(8,128)(2,1)S(1)} %get-tuple-element.101.refs_3_, ...), custom_call_target="tpu_custom_call" | custom-call | flops 11274289152 | bytes 29360128 | tf_op jit(solution)/shard_map/forward_part/pallas_call | solution.py:50
  68.2 11.1 %forward_part.4 = (f32[384,1792]{1,0:T(8,128)S(1)}, f32[384,1792]{1,0:T(8,128)S(1)}, f32[8,128]{1,0:T(8,128)S(1)}) custom-call(s32[2]{0:T(128)S(1)} %get-tuple-element.202.refs_0_, bf16[384,1024]{1,0:T(8,128)(2,1)S(1)} %get-tuple-element.105.refs_1_, bf16[384,1024]{1,0:T(8,128)(2,1)S(1)} %collective-permute-done.9.refs_2_, bf16[8192,1792]{1,0:T(8,128)(2,1)} %refs_5_.15, ...), custom_call_target="tpu_custom_call" | custom-call | flops 5637144576 | bytes 14680064 | tf_op jit(solution)/shard_map/forward_part/pallas_call | solution.py:50
  86.7 3.7 collective-permute-done.8.refs_1_
  97.9 2.6 collective-permute-start.15
  105.4 11.1 %forward_part.5 = (f32[384,1792]{1,0:T(8,128)S(1)}, f32[384,1792]{1,0:T(8,128)S(1)}, f32[8,128]{1,0:T(8,128)S(1)}) custom-call(s32[2]{0:T(128)S(1)} %get-tuple-element.203.refs_0_, bf16[384,1024]{1,0:T(8,128)(2,1)S(1)} %get-tuple-element.115.refs_1_, bf16[384,1024]{1,0:T(8,128)(2,1)S(1)} %collective-permute-done.11.refs_2_, bf16[8192,1792]{1,0:T(8,128)(2,1)} %refs_5_.15, ...), custom_call_target="tpu_custom_call" | custom-call | flops 5637144576 | bytes 14680064 | tf_op jit(solution)/shard_map/forward_part/pallas_call | solution.py:50
  125.1 2.7 activate.1
  131.6 5.9 %mixed_parts.2 = (bf16[1,384,1024]{2,1,0:T(8,128)(2,1)S(1)}, bf16[1,384,1024]{2,1,0:T(8,128)(2,1)S(1)}, f32[8,128]{1,0:T(8,128)S(1)}) custom-call(s32[2]{0:T(128)S(1)} %get-tuple-element.201.refs_0_, bf16[384,1792]{1,0:T(8,128)(2,1)S(1)} %get-tuple-element.125.refs_1_, bf16[1792,8192]{1,0:T(8,128)(2,1)} %refs_8_.5, bf16[1792,8192]{1,0:T(8,128)(2,1)} %refs_8_.5, ...), custom_call_target="tpu_custom_call" | custom-call | flops 2818572288 | bytes 7340032 | tf_op jit(solution)/shard_map/mixed_parts/pallas_call | solution.py:50
  137.6 14.6 %mixed_parts.3 = (bf16[3,384,1024]{2,1,0:T(8,128)(2,1)S(1)}, bf16[3,384,1024]{2,1,0:T(8,128)(2,1)}, f32[8,128]{1,0:T(8,128)S(1)}) custom-call(s32[6]{0:T(128)S(1)} %slice.62.refs_0_, bf16[384,1792]{1,0:T(8,128)(2,1)S(1)} %get-tuple-element.125.refs_1_, bf16[1792,8192]{1,0:T(8,128)(2,1)} %refs_8_.5, bf16[1792,8192]{1,0:T(8,128)(2,1)} %refs_8_.5, ...), custom_call_target="tpu_custom_call" | custom-call | flops 8455716864 | bytes 22020096 | tf_op jit(solution)/shard_map/mixed_parts/pallas_call | solution.py:50
  160.3 11.3 %collective-permute-start.21 = (bf16[384,1024]{1,0:T(8,128)(2,1)}, bf16[384,1024]{1,0:T(8,128)(2,1)}, u32[]{:S(2)}, u32[]{:S(2)}) collective-permute-start(bf16[384,1024]{1,0:T(8,128)(2,1)} %get-tuple-element.139), channel_id=1, source_target_pairs={{0,2},{1,3},{6,4},{7,5},{8,10},{9,11},{14,12},{15,13},{16,18},{17,... | collective-permute-start | bytes 2359304 | tf_op jit(solution)/shard_map/ppermute | solution.py:587
  171.6 10.9 %hidden_part.1 = (f32[384,1792]{1,0:T(8,128)S(1)}, f32[8,128]{1,0:T(8,128)S(1)}) custom-call(s32[4]{0:T(128)S(1)} %slice.66.refs_0_, bf16[384,1024]{1,0:T(8,128)(2,1)S(1)} %copy-done.37, bf16[384,1024]{1,0:T(8,128)(2,1)S(1)} %collective-permute-done.23.refs_2_, bf16[384,1024]{1,0:T(8,128)(2,1)S(1)} %get-tuple-element.141.refs_3_, ...), custom_call_target="tpu_custom_call" | custom-call | flops 5637144576 | bytes 14680064 | tf_op jit(solution)/shard_map/hidden_part/pallas_call | solution.py:50
  189.2 3.9 %line_sums.9 = (bf16[384,1024]{1,0:T(8,128)(2,1)}, bf16[384,1024]{1,0:T(8,128)(2,1)}, f32[8,128]{1,0:T(8,128)S(1)}) custom-call(s32[4]{0:T(128)S(1)} %fusion.3.refs_0_, bf16[1,384,1024]{2,1,0:T(8,128)(2,1)S(1)} %get-tuple-element.132.refs_1_.refs_5_, bf16[1,384,1024]{2,1,0:T(8,128)(2,1)S(1)} %copy-done.7, ...), custom_call_target="tpu_custom_call" | custom-call | flops 134217728 | bytes 349525 | tf_op jit(solution)/shard_map/line_sums/pallas_call | solution.py:50
  193.2 5.3 %collective-permute-start.25 = (bf16[384,1024]{1,0:T(8,128)(2,1)}, bf16[384,1024]{1,0:T(8,128)(2,1)}, u32[]{:S(2)}, u32[]{:S(2)}) collective-permute-start(bf16[384,1024]{1,0:T(8,128)(2,1)} %get-tuple-element.145), channel_id=1, source_target_pairs={{0,2},{1,3},{2,4},{3,5},{8,10},{9,11},{10,12},{11,13},{16,18},{17,... | collective-permute-start | bytes 2359304 | tf_op jit(solution)/shard_map/ppermute | solution.py:589
  200.3 14.1 %hidden_gradients.1 = (bf16[384,1792]{1,0:T(8,128)(2,1)S(1)}, bf16[384,1792]{1,0:T(8,128)(2,1)S(1)}, f32[384,64]{1,0:T(8,128)S(1)}, bf16[3,64,1792]{2,1,0:T(8,128)(2,1)S(1)}, f32[8,128]{1,0:T(8,128)S(1)}) custom-call(s32[4]{0:T(128)S(1)} %slice.72.refs_0_, bf16[384,1024]{1,0:T(8,128)(2,1)} %get-tuple-element.140.refs_1_, ...), custom_call_target="tpu_custom_call" | custom-call | flops 5637144576 | bytes 14680064 | tf_op jit(solution)/shard_map/hidden_gradients/pallas_call | solution.py:50
  220.7 2.9 line_sums.10
  223.7 6.2 %item_part.5 = (bf16[1,384,1024]{2,1,0:T(8,128)(2,1)S(1)}, f32[8,128]{1,0:T(8,128)S(1)}) custom-call(s32[1]{0:T(128)} %get-tuple-element.219.refs_0_, bf16[384,1792]{1,0:T(8,128)(2,1)S(1)} %copy-done.1, bf16[384,1792]{1,0:T(8,128)(2,1)S(1)} %copy-done.4, bf16[8192,1792]{1,0:T(8,128)(2,1)} %refs_5_.15, bf16[8192,1792]{1,0:T(8,128)(2,1)} %refs_6_.15, ...), custom_call_target="tpu_custom_call" | custom-call | flops 2818572288 | bytes 7340032 | tf_op jit(solution)/shard_map/item_part/pallas_call | solution.py:50
  232.7 4.0 %collective-permute-start.29 = (bf16[384,1024]{1,0:T(8,128)(2,1)S(1)}, bf16[384,1024]{1,0:T(8,128)(2,1)S(1)}, u32[]{:S(2)}, u32[]{:S(2)}) collective-permute-start(bf16[384,1024]{1,0:T(8,128)(2,1)S(1)} %get-tuple-element.153), channel_id=1, source_target_pairs={{0,2},{1,3},{2,4},{3,5},{4,6},{5,7},{8,10},{9,11},{10,12},{11,13},... | collective-permute-start | bytes 2359304 | tf_op jit(solution)/shard_map/ppermute | solution.py:589
  237.9 6.0 %item_part.6 = (bf16[1,384,1024]{2,1,0:T(8,128)(2,1)S(1)}, f32[8,128]{1,0:T(8,128)S(1)}) custom-call(s32[1]{0:T(128)} %get-tuple-element.218.refs_0_, bf16[384,1792]{1,0:T(8,128)(2,1)S(1)} %copy-done.1, bf16[384,1792]{1,0:T(8,128)(2,1)S(1)} %copy-done.4, bf16[8192,1792]{1,0:T(8,128)(2,1)} %refs_5_.15, bf16[8192,1792]{1,0:T(8,128)(2,1)} %refs_6_.15, ...), custom_call_target="tpu_custom_call" | custom-call | flops 2818572288 | bytes 7340032 | tf_op jit(solution)/shard_map/item_part/pallas_call | solution.py:50
  244.8 10.0 %item_part.7 = (bf16[1,384,1024]{2,1,0:T(8,128)(2,1)S(1)}, bf16[1,384,1024]{2,1,0:T(8,128)(2,1)S(1)}, f32[8,128]{1,0:T(8,128)S(1)}) custom-call(s32[2]{0:T(128)S(1)} %get-tuple-element.200.refs_0_, bf16[384,1792]{1,0:T(8,128)(2,1)S(1)} %copy-done.1, bf16[384,1792]{1,0:T(8,128)(2,1)S(1)} %copy-done.4, bf16[8192,1792]{1,0:T(8,128)(2,1)} %refs_5_.15, ...), custom_call_target="tpu_custom_call" | custom-call | flops 5637144576 | bytes 14680064 | tf_op jit(solution)/shard_map/item_part/pallas_call | solution.py:50
  254.9 5.1 %collective-permute-start.36 = (bf16[384,1024]{1,0:T(8,128)(2,1)S(1)}, bf16[384,1024]{1,0:T(8,128)(2,1)S(1)}, u32[]{:S(2)}, u32[]{:S(2)}) collective-permute-start(bf16[384,1024]{1,0:T(8,128)(2,1)S(1)} %get-tuple-element.173), channel_id=1, source_target_pairs={{0,2},{1,3},{6,4},{7,5},{8,10},{9,11},{14,12},{15,13},{16,18},{17,... | collective-permute-start | bytes 2359304 | tf_op jit(solution)/shard_map/ppermute | solution.py:587
  260.1 21.5 %collective-permute-done.33.refs_4_ = f32[384,64]{1,0:T(8,128)S(1)} collective-permute-done((f32[384,64]{1,0:T(8,128)S(1)}, f32[384,64]{1,0:T(8,128)S(1)}, u32[]{:S(2)}, u32[]{:S(2)}) %collective-permute-start.33) | collective-permute-done | bytes 98336 | tf_op jit(solution)/shard_map/ppermute | solution.py:623
  283.8 2.8 line_sums.12
  288.9 10.7 %item_part.8 = (bf16[1,384,1024]{2,1,0:T(8,128)(2,1)S(1)}, bf16[1,384,1024]{2,1,0:T(8,128)(2,1)}, f32[8,128]{1,0:T(8,128)S(1)}) custom-call(s32[2]{0:T(128)S(1)} %copy-done.47, bf16[384,1792]{1,0:T(8,128)(2,1)S(1)} %copy-done.1, bf16[384,1792]{1,0:T(8,128)(2,1)S(1)} %copy-done.4, bf16[8192,1792]{1,0:T(8,128)(2,1)} %refs_5_.15, bf16[8192,1792]{1,0:T(8,128)(2,1)} %refs_6_.15, ...), custom_call_target="tpu_custom_call" | custom-call | flops 5637144576 | bytes 14680064 | tf_op jit(solution)/shard_map/item_part/pallas_call | solution.py:50
  300.5 4.4 %collective-permute-start.38 = (bf16[384,1024]{1,0:T(8,128)(2,1)}, bf16[384,1024]{1,0:T(8,128)(2,1)}, u32[]{:S(2)}, u32[]{:S(2)}) collective-permute-start(bf16[384,1024]{1,0:T(8,128)(2,1)} %get-tuple-element.178), channel_id=1, source_target_pairs={{0,2},{1,3},{2,4},{3,5},{8,10},{9,11},{10,12},{11,13},{16,18},{17,... | collective-permute-start | bytes 2359304 | tf_op jit(solution)/shard_map/ppermute | solution.py:589
  312.7 3.1 slot_sums.2
  322.1 3.8 %line_sums.14 = (bf16[384,1024]{1,0:T(8,128)(2,1)}, bf16[384,1024]{1,0:T(8,128)(2,1)}, f32[8,128]{1,0:T(8,128)S(1)}) custom-call(s32[4]{0:T(128)S(1)} %copy-done.50, bf16[1,384,1024]{2,1,0:T(8,128)(2,1)S(1)} %copy-done.10, bf16[1,384,1024]{2,1,0:T(8,128)(2,1)S(1)} %collective-permute-done.34.refs_2_.refs_6_.refs_8_, bf16[1,384,1024]{2,1,0:T(8,128)(2,1)S(1)} %copy-done.12, ...), custom_call_target="tpu_custom_call" | custom-call | flops 134217728 | bytes 349525 | tf_op jit(solution)/shard_map/line_sums/pallas_call | solution.py:50
  325.9 10.7 %item_part.9 = (bf16[1,384,1024]{2,1,0:T(8,128)(2,1)S(1)}, bf16[1,384,1024]{2,1,0:T(8,128)(2,1)}, f32[8,128]{1,0:T(8,128)S(1)}) custom-call(s32[2]{0:T(128)S(1)} %get-tuple-element.199.refs_0_, bf16[384,1792]{1,0:T(8,128)(2,1)S(1)} %copy-done.2, bf16[384,1792]{1,0:T(8,128)(2,1)S(1)} %copy-done.5, bf16[8192,1792]{1,0:T(8,128)(2,1)} %refs_5_.15, ...), custom_call_target="tpu_custom_call" | custom-call | flops 5637144576 | bytes 14680064 | tf_op jit(solution)/shard_map/item_part/pallas_call | solution.py:50
  336.6 8.1 %collective-permute-start.43 = (bf16[384,1024]{1,0:T(8,128)(2,1)}, bf16[384,1024]{1,0:T(8,128)(2,1)S(1)}, u32[]{:S(2)}, u32[]{:S(2)}) collective-permute-start(bf16[384,1024]{1,0:T(8,128)(2,1)} %get-tuple-element.188), channel_id=1, source_target_pairs={{0,2},{1,3},{2,4},{3,5},{4,6},{5,7},{8,10},{9,11},{10,12},{11,13},... | collective-permute-start | bytes 2359304 | tf_op jit(solution)/shard_map/ppermute | solution.py:589
  347.6 2.3 slot_sums.3
  349.9 12.5 %collective-permute-done.43.refs_3_ = bf16[384,1024]{1,0:T(8,128)(2,1)S(1)} collective-permute-done((bf16[384,1024]{1,0:T(8,128)(2,1)}, bf16[384,1024]{1,0:T(8,128)(2,1)S(1)}, u32[]{:S(2)}, u32[]{:S(2)}) %collective-permute-start.43) | collective-permute-done | bytes 786464 | tf_op jit(solution)/shard_map/ppermute | solution.py:589
  362.4 4.1 %collective-permute-done.44.refs_4_ = bf16[384,1024]{1,0:T(8,128)(2,1)S(1)} collective-permute-done((bf16[384,1024]{1,0:T(8,128)(2,1)}, bf16[384,1024]{1,0:T(8,128)(2,1)S(1)}, u32[]{:S(2)}, u32[]{:S(2)}) %collective-permute-start.44) | collective-permute-done | bytes 786464 | tf_op jit(solution)/shard_map/ppermute | solution.py:589
  (263 shorter events, 113.2 us)
Async XLA Ops:
  7.2 75.4 %reduce-scatter.7.cloned.1.call-start = ((), (), s32[]{:S(2)}) async-start(), calls=%async_computation.3 | async-start | bytes 1966080
  7.2 22.7 %collective-permute-start = (bf16[384,1024]{1,0:T(8,128)(2,1)}, bf16[384,1024]{1,0:T(8,128)(2,1)S(1)}, u32[]{:S(2)}, u32[]{:S(2)}) collective-permute-start(bf16[384,1024]{1,0:T(8,128)(2,1)} %refs_1_.5), channel_id=1, source_target_pairs={{2,0},{3,1},{4,2},{5,3},{6,4},{7,5},{10,8},{11,9},{12,10},{13,11},... | collective-permute-start | bytes 2359304 | tf_op jit(solution)/shard_map/ppermute | solution.py:535
  8.5 22.7 %collective-permute-start.2 = (bf16[384,1024]{1,0:T(8,128)(2,1)}, bf16[384,1024]{1,0:T(8,128)(2,1)S(1)}, u32[]{:S(2)}, u32[]{:S(2)}) collective-permute-start(bf16[384,1024]{1,0:T(8,128)(2,1)} %refs_1_.5), channel_id=1, source_target_pairs={{0,2},{1,3},{2,4},{3,5},{4,6},{5,7},{8,10},{9,11},{10,12},{11,13},... | collective-permute-start | bytes 2359304 | tf_op jit(solution)/shard_map/ppermute | solution.py:534
  39.4 81.1 %reduce-scatter.9.cloned.1.call-start = ((), (), s32[]{:S(2)}) async-start(), calls=%async_computation.4 | async-start | bytes 3440640
  40.1 270.7 %all-gather.2.cloned.1.call-start = ((), (), s32[]{:S(2)}) async-start(), calls=%async_computation.2 | async-start | bytes 3440640 | tf_op jit(solution)/shard_map/all_gather | solution.py:714
  43.2 22.0 %collective-permute-start.1 = (bf16[384,1024]{1,0:T(8,128)(2,1)S(1)}, bf16[384,1024]{1,0:T(8,128)(2,1)S(1)}, u32[]{:S(2)}, u32[]{:S(2)}) collective-permute-start(bf16[384,1024]{1,0:T(8,128)(2,1)S(1)} %collective-permute-done.refs_1_.refs_3_), channel_id=1, source_target_pairs={{2,0},{3,1},{4,2},{5,3},{10,8},{11,9},{12,10},{13,11},{18,16},{19,... | collective-permute-start | bytes 2359304 | tf_op jit(solution)/shard_map/ppermute | solution.py:535
  44.4 20.7 %collective-permute-start.3 = (bf16[384,1024]{1,0:T(8,128)(2,1)S(1)}, bf16[384,1024]{1,0:T(8,128)(2,1)S(1)}, u32[]{:S(2)}, u32[]{:S(2)}) collective-permute-start(bf16[384,1024]{1,0:T(8,128)(2,1)S(1)} %collective-permute-done.2.refs_2_), channel_id=1, source_target_pairs={{2,4},{3,5},{4,6},{5,7},{10,12},{11,13},{12,14},{13,15},{18,20},{1... | collective-permute-start | bytes 2359304 | tf_op jit(solution)/shard_map/ppermute | solution.py:534
  66.0 24.4 %collective-permute-start.8 = (bf16[384,1024]{1,0:T(8,128)(2,1)S(1)}, bf16[384,1024]{1,0:T(8,128)(2,1)}, u32[]{:S(2)}, u32[]{:S(2)}) collective-permute-start(bf16[384,1024]{1,0:T(8,128)(2,1)S(1)} %get-tuple-element.105.refs_1_), channel_id=1, source_target_pairs={{4,6},{5,7},{2,0},{3,1},{12,14},{13,15},{10,8},{11,9},{20,22},{21,... | collective-permute-start | bytes 2359304 | tf_op jit(solution)/shard_map/ppermute | solution.py:540
  93.5 26.2 %collective-permute-start.12 = (f32[384,64]{1,0:T(8,128)S(1)}, f32[384,64]{1,0:T(8,128)S(1)}, u32[]{:S(2)}, u32[]{:S(2)}) collective-permute-start(f32[384,64]{1,0:T(8,128)S(1)} %get-tuple-element.121.refs_0_), channel_id=1, source_target_pairs={{0,2},{1,3},{2,0},{3,1},{4,6},{5,7},{6,4},{7,5},{8,10},{9,11},{10,... | collective-permute-start | bytes 294920 | tf_op jit(solution)/shard_map/ppermute | solution.py:623
  95.1 24.6 %collective-permute-start.13 = (f32[384,64]{1,0:T(8,128)S(1)}, f32[384,64]{1,0:T(8,128)S(1)}, u32[]{:S(2)}, u32[]{:S(2)}) collective-permute-start(f32[384,64]{1,0:T(8,128)S(1)} %get-tuple-element.121.refs_0_), channel_id=1, source_target_pairs={{0,4},{1,5},{2,6},{3,7},{4,0},{5,1},{6,2},{7,3},{8,12},{9,13},{10,... | collective-permute-start | bytes 294920 | tf_op jit(solution)/shard_map/ppermute | solution.py:623
  96.2 23.5 %collective-permute-start.14 = (f32[384,64]{1,0:T(8,128)S(1)}, f32[384,64]{1,0:T(8,128)S(1)}, u32[]{:S(2)}, u32[]{:S(2)}) collective-permute-start(f32[384,64]{1,0:T(8,128)S(1)} %get-tuple-element.121.refs_0_), channel_id=1, source_target_pairs={{0,6},{1,7},{2,4},{3,5},{4,2},{5,3},{6,0},{7,1},{8,14},{9,15},{10,... | collective-permute-start | bytes 294920 | tf_op jit(solution)/shard_map/ppermute | solution.py:623
  97.9 30.0 %collective-permute-start.15 = (bf16[384,1024]{1,0:T(8,128)(2,1)S(1)}, bf16[384,1024]{1,0:T(8,128)(2,1)S(1)}, u32[]{:S(2)}, u32[]{:S(2)}) collective-permute-start(bf16[384,1024]{1,0:T(8,128)(2,1)S(1)} %get-tuple-element.126.refs_1_), channel_id=1, source_target_pairs={{0,2},{1,3},{2,4},{3,5},{4,6},{5,7},{8,10},{9,11},{10,12},{11,13},... | collective-permute-start | bytes 2359304 | tf_op jit(solution)/shard_map/ppermute | solution.py:534
  100.5 27.3 %collective-permute-start.16 = (bf16[384,1024]{1,0:T(8,128)(2,1)S(1)}, bf16[384,1024]{1,0:T(8,128)(2,1)}, u32[]{:S(2)}, u32[]{:S(2)}) collective-permute-start(bf16[384,1024]{1,0:T(8,128)(2,1)S(1)} %get-tuple-element.126.refs_1_), channel_id=1, source_target_pairs={{2,0},{3,1},{4,2},{5,3},{6,4},{7,5},{10,8},{11,9},{12,10},{13,11},... | collective-permute-start | bytes 2359304 | tf_op jit(solution)/shard_map/ppermute | solution.py:535
  129.6 23.8 %collective-permute-start.19 = (bf16[384,1024]{1,0:T(8,128)(2,1)S(1)}, bf16[384,1024]{1,0:T(8,128)(2,1)S(1)}, u32[]{:S(2)}, u32[]{:S(2)}) collective-permute-start(bf16[384,1024]{1,0:T(8,128)(2,1)S(1)} %get-tuple-element.134.refs_1_.refs_3_), channel_id=1, source_target_pairs={{2,0},{3,1},{4,2},{5,3},{10,8},{11,9},{12,10},{13,11},{18,16},{19,... | collective-permute-start | bytes 2359304 | tf_op jit(solution)/shard_map/ppermute | solution.py:535
  130.9 23.1 %collective-permute-start.20 = (bf16[384,1024]{1,0:T(8,128)(2,1)S(1)}, bf16[384,1024]{1,0:T(8,128)(2,1)S(1)}, u32[]{:S(2)}, u32[]{:S(2)}) collective-permute-start(bf16[384,1024]{1,0:T(8,128)(2,1)S(1)} %get-tuple-element.135.refs_2_), channel_id=1, source_target_pairs={{2,4},{3,5},{4,6},{5,7},{10,12},{11,13},{12,14},{13,15},{18,20},{1... | collective-permute-start | bytes 2359304 | tf_op jit(solution)/shard_map/ppermute | solution.py:534
  152.2 35.9 %collective-permute-start.17 = (bf16[3,384,1024]{2,1,0:T(8,128)(2,1)}, bf16[3,384,1024]{2,1,0:T(8,128)(2,1)}, u32[]{:S(2)}, u32[]{:S(2)}) collective-permute-start(bf16[3,384,1024]{2,1,0:T(8,128)(2,1)} %get-tuple-element.131), channel_id=1, source_target_pairs={{0,1},{1,0},{2,3},{3,2},{4,5},{5,4},{6,7},{7,6},{8,9},{9,8},{10,11... | collective-permute-start | bytes 7077896 | tf_op jit(solution)/shard_map/ppermute | solution.py:521
  153.5 18.1 %collective-permute-start.24 = (bf16[384,1024]{1,0:T(8,128)(2,1)S(1)}, bf16[384,1024]{1,0:T(8,128)(2,1)S(1)}, u32[]{:S(2)}, u32[]{:S(2)}) collective-permute-start(bf16[384,1024]{1,0:T(8,128)(2,1)S(1)} %get-tuple-element.141.refs_3_), channel_id=1, source_target_pairs={{0,1},{1,0},{2,3},{3,2},{4,5},{5,4},{6,7},{7,6},{8,9},{9,8},{10,11... | collective-permute-start | bytes 2359304 | tf_op jit(solution)/shard_map/ppermute | solution.py:521
  155.6 28.4 %collective-permute-start.22 = (bf16[384,1024]{1,0:T(8,128)(2,1)}, bf16[384,1024]{1,0:T(8,128)(2,1)S(1)}, u32[]{:S(2)}, u32[]{:S(2)}) collective-permute-start(bf16[384,1024]{1,0:T(8,128)(2,1)} %get-tuple-element.140.refs_1_), channel_id=1, source_target_pairs={{4,6},{5,7},{2,0},{3,1},{12,14},{13,15},{10,8},{11,9},{20,22},{21,... | collective-permute-start | bytes 2359304 | tf_op jit(solution)/shard_map/ppermute | solution.py:540
  157.5 42.8 %collective-permute-start.27 = (bf16[384,1024]{1,0:T(8,128)(2,1)}, bf16[384,1024]{1,0:T(8,128)(2,1)}, u32[]{:S(2)}, u32[]{:S(2)}) collective-permute-start(bf16[384,1024]{1,0:T(8,128)(2,1)} %get-tuple-element.140.refs_1_), channel_id=1, source_target_pairs={{0,1},{1,0},{2,3},{3,2},{4,5},{5,4},{6,7},{7,6},{8,9},{9,8},{10,11... | collective-permute-start | bytes 2359304 | tf_op jit(solution)/shard_map/ppermute | solution.py:521
  160.3 27.8 %collective-permute-start.21 = (bf16[384,1024]{1,0:T(8,128)(2,1)}, bf16[384,1024]{1,0:T(8,128)(2,1)}, u32[]{:S(2)}, u32[]{:S(2)}) collective-permute-start(bf16[384,1024]{1,0:T(8,128)(2,1)} %get-tuple-element.139), channel_id=1, source_target_pairs={{0,2},{1,3},{6,4},{7,5},{8,10},{9,11},{14,12},{15,13},{16,18},{17,... | collective-permute-start | bytes 2359304 | tf_op jit(solution)/shard_map/ppermute | solution.py:587
  193.2 26.4 %collective-permute-start.25 = (bf16[384,1024]{1,0:T(8,128)(2,1)}, bf16[384,1024]{1,0:T(8,128)(2,1)}, u32[]{:S(2)}, u32[]{:S(2)}) collective-permute-start(bf16[384,1024]{1,0:T(8,128)(2,1)} %get-tuple-element.145), channel_id=1, source_target_pairs={{0,2},{1,3},{2,4},{3,5},{8,10},{9,11},{10,12},{11,13},{16,18},{17,... | collective-permute-start | bytes 2359304 | tf_op jit(solution)/shard_map/ppermute | solution.py:589
  198.5 21.1 %collective-permute-start.26 = (bf16[384,1024]{1,0:T(8,128)(2,1)}, bf16[384,1024]{1,0:T(8,128)(2,1)}, u32[]{:S(2)}, u32[]{:S(2)}) collective-permute-start(bf16[384,1024]{1,0:T(8,128)(2,1)} %get-tuple-element.146), channel_id=1, source_target_pairs={{4,2},{5,3},{6,4},{7,5},{12,10},{13,11},{14,12},{15,13},{20,18},{2... | collective-permute-start | bytes 2359304 | tf_op jit(solution)/shard_map/ppermute | solution.py:589
  232.7 51.1 %collective-permute-start.29 = (bf16[384,1024]{1,0:T(8,128)(2,1)S(1)}, bf16[384,1024]{1,0:T(8,128)(2,1)S(1)}, u32[]{:S(2)}, u32[]{:S(2)}) collective-permute-start(bf16[384,1024]{1,0:T(8,128)(2,1)S(1)} %get-tuple-element.153), channel_id=1, source_target_pairs={{0,2},{1,3},{2,4},{3,5},{4,6},{5,7},{8,10},{9,11},{10,12},{11,13},... | collective-permute-start | bytes 2359304 | tf_op jit(solution)/shard_map/ppermute | solution.py:589
  236.6 47.2 %collective-permute-start.30 = (bf16[384,1024]{1,0:T(8,128)(2,1)S(1)}, bf16[384,1024]{1,0:T(8,128)(2,1)S(1)}, u32[]{:S(2)}, u32[]{:S(2)}) collective-permute-start(bf16[384,1024]{1,0:T(8,128)(2,1)S(1)} %get-tuple-element.154), channel_id=1, source_target_pairs={{2,0},{3,1},{4,2},{5,3},{6,4},{7,5},{10,8},{11,9},{12,10},{13,11},... | collective-permute-start | bytes 2359304 | tf_op jit(solution)/shard_map/ppermute | solution.py:589
  254.8 31.8 %collective-permute-start.35 = (bf16[1,384,1024]{2,1,0:T(8,128)(2,1)S(1)}, bf16[1,384,1024]{2,1,0:T(8,128)(2,1)S(1)}, u32[]{:S(2)}, u32[]{:S(2)}) collective-permute-start(bf16[1,384,1024]{2,1,0:T(8,128)(2,1)S(1)} %get-tuple-element.172), channel_id=1, source_target_pairs={{0,1},{1,0},{2,3},{3,2},{4,5},{5,4},{6,7},{7,6},{8,9},{9,8},{10,11... | collective-permute-start | bytes 2359304 | tf_op jit(solution)/shard_map/ppermute | solution.py:521
  254.9 31.7 %collective-permute-start.36 = (bf16[384,1024]{1,0:T(8,128)(2,1)S(1)}, bf16[384,1024]{1,0:T(8,128)(2,1)S(1)}, u32[]{:S(2)}, u32[]{:S(2)}) collective-permute-start(bf16[384,1024]{1,0:T(8,128)(2,1)S(1)} %get-tuple-element.173), channel_id=1, source_target_pairs={{0,2},{1,3},{6,4},{7,5},{8,10},{9,11},{14,12},{15,13},{16,18},{17,... | collective-permute-start | bytes 2359304 | tf_op jit(solution)/shard_map/ppermute | solution.py:587
  260.0 21.6 %collective-permute-start.33 = (f32[384,64]{1,0:T(8,128)S(1)}, f32[384,64]{1,0:T(8,128)S(1)}, u32[]{:S(2)}, u32[]{:S(2)}) collective-permute-start(f32[384,64]{1,0:T(8,128)S(1)} %get-tuple-element.163.refs_3_), channel_id=1, source_target_pairs={{0,4},{1,5},{2,6},{3,7},{4,0},{5,1},{6,2},{7,3},{8,12},{9,13},{10,... | collective-permute-start | bytes 294920 | tf_op jit(solution)/shard_map/ppermute | solution.py:623
  300.5 21.5 %collective-permute-start.37 = (bf16[1,384,1024]{2,1,0:T(8,128)(2,1)}, bf16[1,384,1024]{2,1,0:T(8,128)(2,1)}, u32[]{:S(2)}, u32[]{:S(2)}) collective-permute-start(bf16[1,384,1024]{2,1,0:T(8,128)(2,1)} %get-tuple-element.177), channel_id=1, source_target_pairs={{0,1},{1,0},{2,3},{3,2},{4,5},{5,4},{6,7},{7,6},{8,9},{9,8},{10,11... | collective-permute-start | bytes 2359304 | tf_op jit(solution)/shard_map/ppermute | solution.py:521
  300.5 21.5 %collective-permute-start.38 = (bf16[384,1024]{1,0:T(8,128)(2,1)}, bf16[384,1024]{1,0:T(8,128)(2,1)}, u32[]{:S(2)}, u32[]{:S(2)}) collective-permute-start(bf16[384,1024]{1,0:T(8,128)(2,1)} %get-tuple-element.178), channel_id=1, source_target_pairs={{0,2},{1,3},{2,4},{3,5},{8,10},{9,11},{10,12},{11,13},{16,18},{17,... | collective-permute-start | bytes 2359304 | tf_op jit(solution)/shard_map/ppermute | solution.py:589
  321.6 24.6 %collective-permute-start.45 = (bf16[3,64,1024]{2,1,0:T(8,128)(2,1)}, bf16[3,64,1024]{2,1,0:T(8,128)(2,1)}, u32[]{:S(2)}, u32[]{:S(2)}) collective-permute-start(bf16[3,64,1024]{2,1,0:T(8,128)(2,1)} %get-tuple-element.192), channel_id=1, source_target_pairs={{0,8},{8,0},{16,24},{24,16},{1,9},{9,1},{17,25},{25,17},{2,10},{10... | collective-permute-start | bytes 1179656 | tf_op jit(solution)/shard_map/ppermute | solution.py:620
  336.6 25.8 %collective-permute-start.43 = (bf16[384,1024]{1,0:T(8,128)(2,1)}, bf16[384,1024]{1,0:T(8,128)(2,1)S(1)}, u32[]{:S(2)}, u32[]{:S(2)}) collective-permute-start(bf16[384,1024]{1,0:T(8,128)(2,1)} %get-tuple-element.188), channel_id=1, source_target_pairs={{0,2},{1,3},{2,4},{3,5},{4,6},{5,7},{8,10},{9,11},{10,12},{11,13},... | collective-permute-start | bytes 2359304 | tf_op jit(solution)/shard_map/ppermute | solution.py:589
  344.7 21.8 %collective-permute-start.44 = (bf16[384,1024]{1,0:T(8,128)(2,1)}, bf16[384,1024]{1,0:T(8,128)(2,1)S(1)}, u32[]{:S(2)}, u32[]{:S(2)}) collective-permute-start(bf16[384,1024]{1,0:T(8,128)(2,1)} %get-tuple-element.189), channel_id=1, source_target_pairs={{2,0},{3,1},{4,2},{5,3},{6,4},{7,5},{10,8},{11,9},{12,10},{13,11},... | collective-permute-start | bytes 2359304 | tf_op jit(solution)/shard_map/ppermute | solution.py:589
  (78 other events, 664.1 us)
Sparse Core Ops, SparseCore 0:
  39.5 33.1 reduce-scatter.6
  75.7 40.6 reduce-scatter.8
  218.3 39.4 all-gather.1

commit v2 on v1

--- a/solution.py
+++ b/solution.py
@@ -24,7 +24,7 @@
     return next((t for t in range(most, 127, -128) if size % t == 0), size)
 
 
-def ordered_call(kernel, *, grid, in_specs, out_specs, out_shape, name, flops=1 << 27, prefetch=0, scratch=(), after=()):
+def ordered_call(kernel, *, grid, in_specs, out_specs, out_shape, name, flops=1 << 27, prefetch=0, scratch=(), after=(), far=None):
     many = prefetch + len(in_specs)
     outs = len(out_specs)
 
@@ -32,6 +32,9 @@
         mark = refs[many + len(after) + outs]
         mark[...] = jnp.zeros_like(mark)
         kernel(*refs[:many], *refs[many + len(after) : many + len(after) + outs], *refs[many + len(after) + outs + 1 :])
+
+    def shape_of(x):
+        return pltpu.HBM(x.shape, x.dtype) if x.shape == far else x
 
     call = pl.pallas_call(
         run,
@@ -42,12 +45,16 @@
             out_specs=list(out_specs) + [pl.BlockSpec((8, 128), lambda *_: (0, 0))],
             scratch_shapes=list(scratch),
         ),
-        out_shape=list(out_shape) + [jax.ShapeDtypeStruct((8, 128), f32)],
+        out_shape=[shape_of(x) if x.dtype == f32 else x for x in out_shape] + [jax.ShapeDtypeStruct((8, 128), f32)],
         compiler_params=params(),
         cost_estimate=pl.CostEstimate(flops=flops, bytes_accessed=flops // 384, transcendentals=0),
         name=name,
     )
-    return lambda *operands: call(*operands, *after)
+    def place(x):
+        hold = x.shape == far and x.dtype == f32 and name != "activate"
+        return pltpu.with_memory_space_constraint(x, pltpu.HBM) if hold else x
+
+    return lambda *operands: call(*(place(x) for x in operands), *after)
 
 
 def adapter_rows(count):
@@ -121,6 +128,7 @@
             jax.ShapeDtypeStruct((rows, hidden), f32),
         ],
         name="activate",
+        far=(rows, hidden),
         flops=1 << 31,
         after=after,
     )(gate, up, low_b, factor)
@@ -152,6 +160,7 @@
         out_specs=[pl.BlockSpec((rows, tile), lambda t, ids: (0, t))],
         out_shape=[jax.ShapeDtypeStruct((rows, hidden), f32)],
         name="hidden_part",
+        far=(rows, hidden),
         flops=2 * many * rows * width * hidden,
         after=after,
     )(ids, *shards, *([down_weight] * many))
@@ -198,6 +207,7 @@
             jax.ShapeDtypeStruct((count, rank, hidden), bf16),
         ],
         name="hidden_gradients",
+        far=(rows, hidden),
         flops=2 * many * rows * width * hidden,
         after=after,
     )(ids, *shards, *([down_weight] * many), total, act, slope, low_b, factor)
@@ -433,7 +443,6 @@
         out_specs=[block, whole],
         out_shape=[jax.ShapeDtypeStruct(factor.shape, bf16), jax.ShapeDtypeStruct((rows, width), f32)],
         name="low_rank_gradients",
-        flops=COVER,
         after=after,
     )(fill, tokens, factor, *lows)
 
@@ -591,7 +600,7 @@
 
 def scatter_end(part, received, extra, after):
     entry = part[0].shape[0] - 1
-    return line_sums(jnp.array([0, entry], jnp.int32), [part], [list(received)], extra, after)
+    return line_sums(jnp.array([0, entry], jnp.int32), [part], [list(received)], extra, after, flops=COVER)
 
 
 def body(
@@ -713,33 +722,35 @@
 
     out_grads = lax.all_gather(out_grad, "dp", axis=0, tiled=True)
     near_low = from_distance(d_low, distances[0])
-    for s in range(3, chips):
-        *payload, mark = scatter_sums(chip, mixed, mixed_hop, s, chips, [mark])
-        mixed_hop = scatter_hop(payload, s, chips)
     theirs, mark = item(slice(1, 2), [mark])
     theirs = swap_cores(theirs, chips)
     d_low, mark = sum_small([d_low, near_low], [mark])
     far_low = from_distance(d_low, distances[1])
     mine, mark = item(slice(0, 1), [mark])
     parts = [(mine, theirs)]
-    for distance in distances[2:]:
-        d_low, mark = sum_small([d_low, far_low], [mark])
-        far_low = from_distance(d_low, distance)
     item_hop = None
     bits = [1 << i for i in range(groups.bit_length() - 1)]
     for j in range(1, chips):
         *payload, mark = scatter_sums(chip, parts, item_hop, j, chips, [mark])
         item_hop = scatter_hop(payload, j, chips)
+        if j == 1:
+            for s in range(3, chips):
+                *payload, mark = scatter_sums(chip, mixed, mixed_hop, s, chips, [mark])
+                mixed_hop = scatter_hop(payload, s, chips)
+            for distance in distances[2:]:
+                d_low, mark = sum_small([d_low, far_low], [mark])
+                far_low = from_distance(d_low, distance)
         mine, theirs, mark = item(slice(2 * j, 2 * j + 2), [mark])
         parts.append((mine, swap_cores(theirs, chips)))
+        after = [mark] + list(item_hop)
         if j == 1:
+            out_sums, mark = slot_sums(places, out_grads, slots, after, flops=COVER)
             in_grad, through, mark = low_rank_gradients(
                 block_fill, [d_low, far_low], tokens, factor_in, [mark]
             )
             in_grads = {0: in_grad} | {bit: exchange(in_grad, bit) for bit in bits}
-            mixed, mark = scatter_end(mixed[-1], mixed_hop, [], [mark])
         if j == 2:
-            out_sums, mark = slot_sums(places, out_grads, slots, [mark])
+            mixed, mark = scatter_end(mixed[-1], mixed_hop, [], after)
             near = copy_small([in_grads[bit] for bit in bits], [mark])
             mark = near[-1]
             in_grads |= dict(zip(bits, near))
@@ -751,7 +762,7 @@
         [lax.dynamic_slice_in_dim(places, (group ^ r) * count, count, 0) for r in range(groups)]
     )
     in_grads = jnp.concatenate([in_grads[r] for r in range(groups)])
-    in_sums, mark = slot_sums(near_places, in_grads, slots, [mark], flops=COVER)
+    in_sums, mark = slot_sums(near_places, in_grads, slots, after, flops=COVER)
     item_derivative = scatter_end(parts[-1], item_hop, [through], [mark])[0]
     return (mixed, item_derivative, in_sums, out_sums)
 

time: 377 us -> 353 us (0.936)
  waiting for transfers between devices: 63.4 us -> 41.3 us
  starting transfers between devices: 76.5 us -> 68.6 us
    ppermute x7, waiting for transfers between devices: 24.2 us -> 2.17 us  [from_distance(): return lax.ppermute(x, 'tensor', [(i, i ^ distance) for i in range(size)])]
    ppermute x4, starting transfers between devices: 21.8 us -> 15.2 us  [scatter_hop(): lax.ppermute(payload[0], 'tensor', up)]
    unnamed x122 -> x126, local copies, waits for them, and re-layouts: 36.4 us -> 41.2 us
  transfers between devices with their start and end apart: 49 -> 49, of which waited for: 16 -> 18; matrix products, arithmetic and copies ran while one was open for 3% -> 3% of each run, Pallas kernels for 44% -> 44%
where the time goes in v2:
time: 353 us; the launch traced here: 351 us
  Pallas kernels  175 us (50%)
  starting transfers between devices  68.6 us (19%)
  local copies, waits for them, and re-layouts  47.6 us (13%)
  waiting for transfers between devices  41.3 us (12%)
  between operations  14.6 us (4%)
  other arithmetic  3.94 us (1%)
    pallas_call x39, Pallas kernels, ordered_call(): return lambda *operands: call(*(place(x) for x in operands), *after)  175 us
    unnamed x126, local copies, waits for them, and re-layouts  41.2 us
    ppermute x4, starting transfers between devices, scatter_hop(): lax.ppermute(payload[0], 'tensor', up)  15.2 us
    ppermute x2, starting transfers between devices, scatter_hop(): both = lax.ppermute(payload[0], 'tensor', up + down)  12.9 us
    ppermute x4, starting transfers between devices, line_hop(): lax.ppermute(left, 'tensor', line_pairs(range(s - 1, chips - 1), 1))  9.66 us
    ppermute x4, waiting for transfers between devices, scatter_hop(): lax.ppermute(payload[0], 'tensor', up)  9.57 us
    ppermute x4, waiting for transfers between devices, line_hop(): lax.ppermute(right, 'tensor', line_pairs(range(1, chips - s + 1), -1))  8.97 us
    ppermute x7, starting transfers between devices, from_distance(): return lax.ppermute(x, 'tensor', [(i, i ^ distance) for i in range(size)])  8.95 us
  transfers between devices with their start and end apart: 49, of which 18 were waited for; matrix products, arithmetic and copies ran while one was open for 3% of the time, Pallas kernels for 44%

profile of v2, /device:TPU:0, one launch (start us, length us, event | category | flops | bytes accessed | tf_op | source)
XLA Modules:
  0.0 350.7 jit_solution(563637920094531531)
XLA Ops:
  8.5 5.6 %collective-permute-start.2 = (bf16[384,1024]{1,0:T(8,128)(2,1)}, bf16[384,1024]{1,0:T(8,128)(2,1)S(1)}, u32[]{:S(2)}, u32[]{:S(2)}) collective-permute-start(bf16[384,1024]{1,0:T(8,128)(2,1)} %refs_1_.5), channel_id=1, source_target_pairs={{0,2},{1,3},{2,4},{3,5},{4,6},{5,7},{8,10},{9,11},{10,12},{11,13},... | collective-permute-start | bytes 2359304 | tf_op jit(solution)/shard_map/ppermute | solution.py:543
  22.4 7.5 %collective-permute-done.refs_1_.refs_3_ = bf16[384,1024]{1,0:T(8,128)(2,1)S(1)} collective-permute-done((bf16[384,1024]{1,0:T(8,128)(2,1)}, bf16[384,1024]{1,0:T(8,128)(2,1)S(1)}, u32[]{:S(2)}, u32[]{:S(2)}) %collective-permute-start) | collective-permute-done | bytes 786464 | tf_op jit(solution)/shard_map/ppermute | solution.py:544
  45.1 18.5 %forward_part.3 = (f32[384,1792]{1,0:T(8,128)S(1)}, f32[384,1792]{1,0:T(8,128)S(1)}, f32[8,128]{1,0:T(8,128)S(1)}) custom-call(s32[4]{0:T(128)S(1)} %slice.66.refs_0_, bf16[384,1024]{1,0:T(8,128)(2,1)S(1)} %copy-done.15, bf16[384,1024]{1,0:T(8,128)(2,1)} %collective-permute-done.4.refs_2_, bf16[384,1024]{1,0:T(8,128)(2,1)S(1)} %get-tuple-element.101.refs_3_, ...), custom_call_target="tpu_custom_call" | custom-call | flops 11274289152 | bytes 29360128 | tf_op jit(solution)/shard_map/forward_part/pallas_call | solution.py:57
  68.1 11.1 %forward_part.4 = (f32[384,1792]{1,0:T(8,128)S(1)}, f32[384,1792]{1,0:T(8,128)S(1)}, f32[8,128]{1,0:T(8,128)S(1)}) custom-call(s32[2]{0:T(128)S(1)} %get-tuple-element.202.refs_0_, bf16[384,1024]{1,0:T(8,128)(2,1)S(1)} %get-tuple-element.105.refs_1_, bf16[384,1024]{1,0:T(8,128)(2,1)S(1)} %collective-permute-done.9.refs_2_, bf16[8192,1792]{1,0:T(8,128)(2,1)} %refs_5_.15, ...), custom_call_target="tpu_custom_call" | custom-call | flops 5637144576 | bytes 14680064 | tf_op jit(solution)/shard_map/forward_part/pallas_call | solution.py:57
  86.5 3.7 %collective-permute-done.8.refs_1_ = bf16[384,1024]{1,0:T(8,128)(2,1)} collective-permute-done((bf16[384,1024]{1,0:T(8,128)(2,1)S(1)}, bf16[384,1024]{1,0:T(8,128)(2,1)}, u32[]{:S(2)}, u32[]{:S(2)}) %collective-permute-start.8) | collective-permute-done | bytes 786464 | tf_op jit(solution)/shard_map/ppermute | solution.py:549
  104.7 11.2 %forward_part.5 = (f32[384,1792]{1,0:T(8,128)S(1)}, f32[384,1792]{1,0:T(8,128)S(1)}, f32[8,128]{1,0:T(8,128)S(1)}) custom-call(s32[2]{0:T(128)S(1)} %get-tuple-element.203.refs_0_, bf16[384,1024]{1,0:T(8,128)(2,1)S(1)} %get-tuple-element.115.refs_1_, bf16[384,1024]{1,0:T(8,128)(2,1)S(1)} %collective-permute-done.11.refs_2_, bf16[8192,1792]{1,0:T(8,128)(2,1)} %refs_5_.15, ...), custom_call_target="tpu_custom_call" | custom-call | flops 5637144576 | bytes 14680064 | tf_op jit(solution)/shard_map/forward_part/pallas_call | solution.py:57
  124.4 5.0 %activate.1 = (bf16[384,1792]{1,0:T(8,128)(2,1)S(1)}, f32[384,1792]{1,0:T(8,128)}, f32[384,1792]{1,0:T(8,128)}, f32[8,128]{1,0:T(8,128)S(1)}) custom-call(f32[384,1792]{1,0:T(8,128)S(1)} %copy-done.48, f32[384,1792]{1,0:T(8,128)S(1)} %copy-done.50, bf16[384,64]{1,0:T(8,128)(2,1)S(1)} %multiply_convert_fusion.refs_2_.refs_12_, ...), custom_call_target="tpu_custom_call" | custom-call | flops 2147483648 | bytes 5592405 | tf_op jit(solution)/shard_map/activate/pallas_call | solution.py:57
  132.7 5.9 %mixed_parts.2 = (bf16[1,384,1024]{2,1,0:T(8,128)(2,1)S(1)}, bf16[1,384,1024]{2,1,0:T(8,128)(2,1)S(1)}, f32[8,128]{1,0:T(8,128)S(1)}) custom-call(s32[2]{0:T(128)S(1)} %get-tuple-element.201.refs_0_, bf16[384,1792]{1,0:T(8,128)(2,1)S(1)} %get-tuple-element.125.refs_1_, bf16[1792,8192]{1,0:T(8,128)(2,1)} %refs_8_.5, bf16[1792,8192]{1,0:T(8,128)(2,1)} %refs_8_.5, ...), custom_call_target="tpu_custom_call" | custom-call | flops 2818572288 | bytes 7340032 | tf_op jit(solution)/shard_map/mixed_parts/pallas_call | solution.py:57
  138.6 14.5 %mixed_parts.3 = (bf16[3,384,1024]{2,1,0:T(8,128)(2,1)S(1)}, bf16[3,384,1024]{2,1,0:T(8,128)(2,1)}, f32[8,128]{1,0:T(8,128)S(1)}) custom-call(s32[6]{0:T(128)S(1)} %slice.62.refs_0_, bf16[384,1792]{1,0:T(8,128)(2,1)S(1)} %get-tuple-element.125.refs_1_, bf16[1792,8192]{1,0:T(8,128)(2,1)} %refs_8_.5, bf16[1792,8192]{1,0:T(8,128)(2,1)} %refs_8_.5, ...), custom_call_target="tpu_custom_call" | custom-call | flops 8455716864 | bytes 22020096 | tf_op jit(solution)/shard_map/mixed_parts/pallas_call | solution.py:57
  161.3 9.6 %collective-permute-start.21 = (bf16[384,1024]{1,0:T(8,128)(2,1)}, bf16[384,1024]{1,0:T(8,128)(2,1)}, u32[]{:S(2)}, u32[]{:S(2)}) collective-permute-start(bf16[384,1024]{1,0:T(8,128)(2,1)} %get-tuple-element.139), channel_id=1, source_target_pairs={{0,2},{1,3},{6,4},{7,5},{8,10},{9,11},{14,12},{15,13},{16,18},{17,... | collective-permute-start | bytes 2359304 | tf_op jit(solution)/shard_map/ppermute | solution.py:596
  170.8 12.1 %hidden_part.1 = (f32[384,1792]{1,0:T(8,128)}, f32[8,128]{1,0:T(8,128)S(1)}) custom-call(s32[4]{0:T(128)S(1)} %slice.66.refs_0_, bf16[384,1024]{1,0:T(8,128)(2,1)S(1)} %copy-done.31, bf16[384,1024]{1,0:T(8,128)(2,1)S(1)} %collective-permute-done.23.refs_2_, bf16[384,1024]{1,0:T(8,128)(2,1)S(1)} %get-tuple-element.141.refs_3_, ...), custom_call_target="tpu_custom_call" | custom-call | flops 5637144576 | bytes 14680064 | tf_op jit(solution)/shard_map/hidden_part/pallas_call | solution.py:57
  188.5 3.0 line_sums.9
  193.3 15.0 %hidden_gradients.1 = (bf16[384,1792]{1,0:T(8,128)(2,1)S(1)}, bf16[384,1792]{1,0:T(8,128)(2,1)S(1)}, f32[384,64]{1,0:T(8,128)S(1)}, bf16[3,64,1792]{2,1,0:T(8,128)(2,1)S(1)}, f32[8,128]{1,0:T(8,128)S(1)}) custom-call(s32[4]{0:T(128)S(1)} %slice.73.refs_0_, bf16[384,1024]{1,0:T(8,128)(2,1)} %get-tuple-element.140.refs_1_, ...), custom_call_target="tpu_custom_call" | custom-call | flops 5637144576 | bytes 14680064 | tf_op jit(solution)/shard_map/hidden_gradients/pallas_call | solution.py:57
  215.5 6.3 %item_part.5 = (bf16[1,384,1024]{2,1,0:T(8,128)(2,1)S(1)}, f32[8,128]{1,0:T(8,128)S(1)}) custom-call(s32[1]{0:T(128)} %get-tuple-element.218.refs_0_, bf16[384,1792]{1,0:T(8,128)(2,1)S(1)} %copy-done.1, bf16[384,1792]{1,0:T(8,128)(2,1)S(1)} %copy-done.5, bf16[8192,1792]{1,0:T(8,128)(2,1)} %refs_5_.15, bf16[8192,1792]{1,0:T(8,128)(2,1)} %refs_6_.15, ...), custom_call_target="tpu_custom_call" | custom-call | flops 2818572288 | bytes 7340032 | tf_op jit(solution)/shard_map/item_part/pallas_call | solution.py:57
  221.9 4.4 %collective-permute-start.25 = (bf16[384,1024]{1,0:T(8,128)(2,1)S(1)}, bf16[384,1024]{1,0:T(8,128)(2,1)S(1)}, u32[]{:S(2)}, u32[]{:S(2)}) collective-permute-start(bf16[384,1024]{1,0:T(8,128)(2,1)S(1)} %copy-done.56), channel_id=1, source_target_pairs={{0,2},{1,3},{2,4},{3,5},{8,10},{9,11},{10,12},{11,13},{16,18},{17,... | collective-permute-start | bytes 2359304 | tf_op jit(solution)/shard_map/ppermute | solution.py:598
  229.3 6.0 %item_part.6 = (bf16[1,384,1024]{2,1,0:T(8,128)(2,1)S(1)}, f32[8,128]{1,0:T(8,128)S(1)}) custom-call(s32[1]{0:T(128)} %get-tuple-element.219.refs_0_, bf16[384,1792]{1,0:T(8,128)(2,1)S(1)} %copy-done.2, bf16[384,1792]{1,0:T(8,128)(2,1)S(1)} %copy-done.5, bf16[8192,1792]{1,0:T(8,128)(2,1)} %refs_5_.15, bf16[8192,1792]{1,0:T(8,128)(2,1)} %refs_6_.15, ...), custom_call_target="tpu_custom_call" | custom-call | flops 2818572288 | bytes 7340032 | tf_op jit(solution)/shard_map/item_part/pallas_call | solution.py:57
  236.2 3.3 collective-permute-start.35
  239.5 4.6 %collective-permute-done.25.refs_9_ = bf16[384,1024]{1,0:T(8,128)(2,1)S(1)} collective-permute-done((bf16[384,1024]{1,0:T(8,128)(2,1)S(1)}, bf16[384,1024]{1,0:T(8,128)(2,1)S(1)}, u32[]{:S(2)}, u32[]{:S(2)}) %collective-permute-start.25) | collective-permute-done | bytes 786464 | tf_op jit(solution)/shard_map/ppermute | solution.py:598
  244.1 3.3 line_sums.11
  248.4 10.7 %item_part.7 = (bf16[1,384,1024]{2,1,0:T(8,128)(2,1)S(1)}, bf16[1,384,1024]{2,1,0:T(8,128)(2,1)}, f32[8,128]{1,0:T(8,128)S(1)}) custom-call(s32[2]{0:T(128)S(1)} %get-tuple-element.199.refs_0_, bf16[384,1792]{1,0:T(8,128)(2,1)S(1)} %copy-done.2, bf16[384,1792]{1,0:T(8,128)(2,1)S(1)} %copy-done.6, bf16[8192,1792]{1,0:T(8,128)(2,1)} %refs_5_.15, ...), custom_call_target="tpu_custom_call" | custom-call | flops 5637144576 | bytes 14680064 | tf_op jit(solution)/shard_map/item_part/pallas_call | solution.py:57
  259.6 3.4 collective-permute-start.36
  271.3 3.1 slot_sums.2
  280.9 4.6 %collective-permute-start.37 = (bf16[384,1024]{1,0:T(8,128)(2,1)S(1)}, bf16[384,1024]{1,0:T(8,128)(2,1)S(1)}, u32[]{:S(2)}, u32[]{:S(2)}) collective-permute-start(bf16[384,1024]{1,0:T(8,128)(2,1)S(1)} %get-tuple-element.177), channel_id=1, source_target_pairs={{0,2},{1,3},{2,4},{3,5},{8,10},{9,11},{10,12},{11,13},{16,18},{17,... | collective-permute-start | bytes 2359304 | tf_op jit(solution)/shard_map/ppermute | solution.py:598
  286.3 10.0 %item_part.8 = (bf16[1,384,1024]{2,1,0:T(8,128)(2,1)S(1)}, bf16[1,384,1024]{2,1,0:T(8,128)(2,1)S(1)}, f32[8,128]{1,0:T(8,128)S(1)}) custom-call(s32[2]{0:T(128)S(1)} %get-tuple-element.200.refs_0_, bf16[384,1792]{1,0:T(8,128)(2,1)S(1)} %copy-done.3, bf16[384,1792]{1,0:T(8,128)(2,1)S(1)} %copy-done.7, bf16[8192,1792]{1,0:T(8,128)(2,1)} %refs_5_.15, ...), custom_call_target="tpu_custom_call" | custom-call | flops 5637144576 | bytes 14680064 | tf_op jit(solution)/shard_map/item_part/pallas_call | solution.py:57
  302.7 3.1 line_sums.13
  305.8 3.0 collective-permute-done.40.refs_0_
  310.8 3.4 line_sums.14
  314.2 3.6 %collective-permute-start.43 = (bf16[384,1024]{1,0:T(8,128)(2,1)}, bf16[384,1024]{1,0:T(8,128)(2,1)S(1)}, u32[]{:S(2)}, u32[]{:S(2)}) collective-permute-start(bf16[384,1024]{1,0:T(8,128)(2,1)} %get-tuple-element.188), channel_id=1, source_target_pairs={{0,2},{1,3},{2,4},{3,5},{4,6},{5,7},{8,10},{9,11},{10,12},{11,13},... | collective-permute-start | bytes 2359304 | tf_op jit(solution)/shard_map/ppermute | solution.py:598
  319.1 10.7 %item_part.9 = (bf16[1,384,1024]{2,1,0:T(8,128)(2,1)S(1)}, bf16[1,384,1024]{2,1,0:T(8,128)(2,1)}, f32[8,128]{1,0:T(8,128)S(1)}) custom-call(s32[2]{0:T(128)S(1)} %get-tuple-element.198.refs_0_, bf16[384,1792]{1,0:T(8,128)(2,1)S(1)} %copy-done.3, bf16[384,1792]{1,0:T(8,128)(2,1)S(1)} %copy-done.7, bf16[8192,1792]{1,0:T(8,128)(2,1)} %refs_5_.15, ...), custom_call_target="tpu_custom_call" | custom-call | flops 5637144576 | bytes 14680064 | tf_op jit(solution)/shard_map/item_part/pallas_call | solution.py:57
  331.2 2.8 collective-permute-done.43.refs_3_
  333.9 4.9 %collective-permute-done.44.refs_4_ = bf16[384,1024]{1,0:T(8,128)(2,1)S(1)} collective-permute-done((bf16[384,1024]{1,0:T(8,128)(2,1)}, bf16[384,1024]{1,0:T(8,128)(2,1)S(1)}, u32[]{:S(2)}, u32[]{:S(2)}) %collective-permute-start.44) | collective-permute-done | bytes 786464 | tf_op jit(solution)/shard_map/ppermute | solution.py:598
  341.1 3.0 line_sums.15
  (267 shorter events, 119.1 us)
Async XLA Ops:
  7.2 75.2 %reduce-scatter.7.cloned.1.call-start = ((), (), s32[]{:S(2)}) async-start(), calls=%async_computation.3 | async-start | bytes 1966080
  7.2 22.7 %collective-permute-start = (bf16[384,1024]{1,0:T(8,128)(2,1)}, bf16[384,1024]{1,0:T(8,128)(2,1)S(1)}, u32[]{:S(2)}, u32[]{:S(2)}) collective-permute-start(bf16[384,1024]{1,0:T(8,128)(2,1)} %refs_1_.5), channel_id=1, source_target_pairs={{2,0},{3,1},{4,2},{5,3},{6,4},{7,5},{10,8},{11,9},{12,10},{13,11},... | collective-permute-start | bytes 2359304 | tf_op jit(solution)/shard_map/ppermute | solution.py:544
  8.5 22.7 %collective-permute-start.2 = (bf16[384,1024]{1,0:T(8,128)(2,1)}, bf16[384,1024]{1,0:T(8,128)(2,1)S(1)}, u32[]{:S(2)}, u32[]{:S(2)}) collective-permute-start(bf16[384,1024]{1,0:T(8,128)(2,1)} %refs_1_.5), channel_id=1, source_target_pairs={{0,2},{1,3},{2,4},{3,5},{4,6},{5,7},{8,10},{9,11},{10,12},{11,13},... | collective-permute-start | bytes 2359304 | tf_op jit(solution)/shard_map/ppermute | solution.py:543
  39.3 80.5 %reduce-scatter.9.cloned.1.call-start = ((), (), s32[]{:S(2)}) async-start(), calls=%async_computation.4 | async-start | bytes 3440640
  40.1 227.6 %all-gather.2.cloned.1.call-start = ((), (), s32[]{:S(2)}) async-start(), calls=%async_computation.2 | async-start | bytes 3440640 | tf_op jit(solution)/shard_map/all_gather | solution.py:723
  43.1 22.0 %collective-permute-start.1 = (bf16[384,1024]{1,0:T(8,128)(2,1)S(1)}, bf16[384,1024]{1,0:T(8,128)(2,1)S(1)}, u32[]{:S(2)}, u32[]{:S(2)}) collective-permute-start(bf16[384,1024]{1,0:T(8,128)(2,1)S(1)} %collective-permute-done.refs_1_.refs_3_), channel_id=1, source_target_pairs={{2,0},{3,1},{4,2},{5,3},{10,8},{11,9},{12,10},{13,11},{18,16},{19,... | collective-permute-start | bytes 2359304 | tf_op jit(solution)/shard_map/ppermute | solution.py:544
  44.4 20.7 %collective-permute-start.3 = (bf16[384,1024]{1,0:T(8,128)(2,1)S(1)}, bf16[384,1024]{1,0:T(8,128)(2,1)S(1)}, u32[]{:S(2)}, u32[]{:S(2)}) collective-permute-start(bf16[384,1024]{1,0:T(8,128)(2,1)S(1)} %collective-permute-done.2.refs_2_), channel_id=1, source_target_pairs={{2,4},{3,5},{4,6},{5,7},{10,12},{11,13},{12,14},{13,15},{18,20},{1... | collective-permute-start | bytes 2359304 | tf_op jit(solution)/shard_map/ppermute | solution.py:543
  65.9 24.4 %collective-permute-start.8 = (bf16[384,1024]{1,0:T(8,128)(2,1)S(1)}, bf16[384,1024]{1,0:T(8,128)(2,1)}, u32[]{:S(2)}, u32[]{:S(2)}) collective-permute-start(bf16[384,1024]{1,0:T(8,128)(2,1)S(1)} %get-tuple-element.105.refs_1_), channel_id=1, source_target_pairs={{4,6},{5,7},{2,0},{3,1},{12,14},{13,15},{10,8},{11,9},{20,22},{21,... | collective-permute-start | bytes 2359304 | tf_op jit(solution)/shard_map/ppermute | solution.py:549
  92.8 26.2 %collective-permute-start.12 = (f32[384,64]{1,0:T(8,128)S(1)}, f32[384,64]{1,0:T(8,128)S(1)}, u32[]{:S(2)}, u32[]{:S(2)}) collective-permute-start(f32[384,64]{1,0:T(8,128)S(1)} %get-tuple-element.121.refs_0_), channel_id=1, source_target_pairs={{0,2},{1,3},{2,0},{3,1},{4,6},{5,7},{6,4},{7,5},{8,10},{9,11},{10,... | collective-permute-start | bytes 294920 | tf_op jit(solution)/shard_map/ppermute | solution.py:632
  94.4 24.6 %collective-permute-start.13 = (f32[384,64]{1,0:T(8,128)S(1)}, f32[384,64]{1,0:T(8,128)S(1)}, u32[]{:S(2)}, u32[]{:S(2)}) collective-permute-start(f32[384,64]{1,0:T(8,128)S(1)} %get-tuple-element.121.refs_0_), channel_id=1, source_target_pairs={{0,4},{1,5},{2,6},{3,7},{4,0},{5,1},{6,2},{7,3},{8,12},{9,13},{10,... | collective-permute-start | bytes 294920 | tf_op jit(solution)/shard_map/ppermute | solution.py:632
  95.5 23.5 %collective-permute-start.14 = (f32[384,64]{1,0:T(8,128)S(1)}, f32[384,64]{1,0:T(8,128)S(1)}, u32[]{:S(2)}, u32[]{:S(2)}) collective-permute-start(f32[384,64]{1,0:T(8,128)S(1)} %get-tuple-element.121.refs_0_), channel_id=1, source_target_pairs={{0,6},{1,7},{2,4},{3,5},{4,2},{5,3},{6,0},{7,1},{8,14},{9,15},{10,... | collective-permute-start | bytes 294920 | tf_op jit(solution)/shard_map/ppermute | solution.py:632
  97.2 32.3 %collective-permute-start.15 = (bf16[384,1024]{1,0:T(8,128)(2,1)S(1)}, bf16[384,1024]{1,0:T(8,128)(2,1)S(1)}, u32[]{:S(2)}, u32[]{:S(2)}) collective-permute-start(bf16[384,1024]{1,0:T(8,128)(2,1)S(1)} %get-tuple-element.126.refs_1_), channel_id=1, source_target_pairs={{0,2},{1,3},{2,4},{3,5},{4,6},{5,7},{8,10},{9,11},{10,12},{11,13},... | collective-permute-start | bytes 2359304 | tf_op jit(solution)/shard_map/ppermute | solution.py:543
  99.8 29.6 %collective-permute-start.16 = (bf16[384,1024]{1,0:T(8,128)(2,1)S(1)}, bf16[384,1024]{1,0:T(8,128)(2,1)}, u32[]{:S(2)}, u32[]{:S(2)}) collective-permute-start(bf16[384,1024]{1,0:T(8,128)(2,1)S(1)} %get-tuple-element.126.refs_1_), channel_id=1, source_target_pairs={{2,0},{3,1},{4,2},{5,3},{6,4},{7,5},{10,8},{11,9},{12,10},{13,11},... | collective-permute-start | bytes 2359304 | tf_op jit(solution)/shard_map/ppermute | solution.py:544
  130.7 23.7 %collective-permute-start.19 = (bf16[384,1024]{1,0:T(8,128)(2,1)S(1)}, bf16[384,1024]{1,0:T(8,128)(2,1)S(1)}, u32[]{:S(2)}, u32[]{:S(2)}) collective-permute-start(bf16[384,1024]{1,0:T(8,128)(2,1)S(1)} %get-tuple-element.134.refs_1_.refs_3_), channel_id=1, source_target_pairs={{2,0},{3,1},{4,2},{5,3},{10,8},{11,9},{12,10},{13,11},{18,16},{19,... | collective-permute-start | bytes 2359304 | tf_op jit(solution)/shard_map/ppermute | solution.py:544
  132.0 23.0 %collective-permute-start.20 = (bf16[384,1024]{1,0:T(8,128)(2,1)S(1)}, bf16[384,1024]{1,0:T(8,128)(2,1)S(1)}, u32[]{:S(2)}, u32[]{:S(2)}) collective-permute-start(bf16[384,1024]{1,0:T(8,128)(2,1)S(1)} %get-tuple-element.135.refs_2_), channel_id=1, source_target_pairs={{2,4},{3,5},{4,6},{5,7},{10,12},{11,13},{12,14},{13,15},{18,20},{1... | collective-permute-start | bytes 2359304 | tf_op jit(solution)/shard_map/ppermute | solution.py:543
  153.2 34.2 %collective-permute-start.17 = (bf16[3,384,1024]{2,1,0:T(8,128)(2,1)}, bf16[3,384,1024]{2,1,0:T(8,128)(2,1)}, u32[]{:S(2)}, u32[]{:S(2)}) collective-permute-start(bf16[3,384,1024]{2,1,0:T(8,128)(2,1)} %get-tuple-element.131), channel_id=1, source_target_pairs={{0,1},{1,0},{2,3},{3,2},{4,5},{5,4},{6,7},{7,6},{8,9},{9,8},{10,11... | collective-permute-start | bytes 7077896 | tf_op jit(solution)/shard_map/ppermute | solution.py:530
  154.4 16.4 %collective-permute-start.24 = (bf16[384,1024]{1,0:T(8,128)(2,1)S(1)}, bf16[384,1024]{1,0:T(8,128)(2,1)S(1)}, u32[]{:S(2)}, u32[]{:S(2)}) collective-permute-start(bf16[384,1024]{1,0:T(8,128)(2,1)S(1)} %get-tuple-element.141.refs_3_), channel_id=1, source_target_pairs={{0,1},{1,0},{2,3},{3,2},{4,5},{5,4},{6,7},{7,6},{8,9},{9,8},{10,11... | collective-permute-start | bytes 2359304 | tf_op jit(solution)/shard_map/ppermute | solution.py:530
  156.5 26.4 %collective-permute-start.22 = (bf16[384,1024]{1,0:T(8,128)(2,1)}, bf16[384,1024]{1,0:T(8,128)(2,1)S(1)}, u32[]{:S(2)}, u32[]{:S(2)}) collective-permute-start(bf16[384,1024]{1,0:T(8,128)(2,1)} %get-tuple-element.140.refs_1_), channel_id=1, source_target_pairs={{4,6},{5,7},{2,0},{3,1},{12,14},{13,15},{10,8},{11,9},{20,22},{21,... | collective-permute-start | bytes 2359304 | tf_op jit(solution)/shard_map/ppermute | solution.py:549
  158.5 34.8 %collective-permute-start.27 = (bf16[384,1024]{1,0:T(8,128)(2,1)}, bf16[384,1024]{1,0:T(8,128)(2,1)}, u32[]{:S(2)}, u32[]{:S(2)}) collective-permute-start(bf16[384,1024]{1,0:T(8,128)(2,1)} %get-tuple-element.140.refs_1_), channel_id=1, source_target_pairs={{0,1},{1,0},{2,3},{3,2},{4,5},{5,4},{6,7},{7,6},{8,9},{9,8},{10,11... | collective-permute-start | bytes 2359304 | tf_op jit(solution)/shard_map/ppermute | solution.py:530
  161.3 26.1 %collective-permute-start.21 = (bf16[384,1024]{1,0:T(8,128)(2,1)}, bf16[384,1024]{1,0:T(8,128)(2,1)}, u32[]{:S(2)}, u32[]{:S(2)}) collective-permute-start(bf16[384,1024]{1,0:T(8,128)(2,1)} %get-tuple-element.139), channel_id=1, source_target_pairs={{0,2},{1,3},{6,4},{7,5},{8,10},{9,11},{14,12},{15,13},{16,18},{17,... | collective-permute-start | bytes 2359304 | tf_op jit(solution)/shard_map/ppermute | solution.py:596
  221.9 22.2 %collective-permute-start.25 = (bf16[384,1024]{1,0:T(8,128)(2,1)S(1)}, bf16[384,1024]{1,0:T(8,128)(2,1)S(1)}, u32[]{:S(2)}, u32[]{:S(2)}) collective-permute-start(bf16[384,1024]{1,0:T(8,128)(2,1)S(1)} %copy-done.56), channel_id=1, source_target_pairs={{0,2},{1,3},{2,4},{3,5},{8,10},{9,11},{10,12},{11,13},{16,18},{17,... | collective-permute-start | bytes 2359304 | tf_op jit(solution)/shard_map/ppermute | solution.py:598
  226.3 17.8 %collective-permute-start.26 = (bf16[384,1024]{1,0:T(8,128)(2,1)S(1)}, bf16[384,1024]{1,0:T(8,128)(2,1)S(1)}, u32[]{:S(2)}, u32[]{:S(2)}) collective-permute-start(bf16[384,1024]{1,0:T(8,128)(2,1)S(1)} %copy-done.54), channel_id=1, source_target_pairs={{4,2},{5,3},{6,4},{7,5},{12,10},{13,11},{14,12},{15,13},{20,18},{2... | collective-permute-start | bytes 2359304 | tf_op jit(solution)/shard_map/ppermute | solution.py:598
  228.6 19.7 %collective-permute-start.33 = (f32[384,64]{1,0:T(8,128)S(1)}, f32[384,64]{1,0:T(8,128)S(1)}, u32[]{:S(2)}, u32[]{:S(2)}) collective-permute-start(f32[384,64]{1,0:T(8,128)S(1)} %get-tuple-element.164.refs_0_), channel_id=1, source_target_pairs={{0,2},{1,3},{2,0},{3,1},{4,6},{5,7},{6,4},{7,5},{8,10},{9,11},{10,... | collective-permute-start | bytes 294920 | tf_op jit(solution)/shard_map/ppermute | solution.py:632
  236.2 30.6 %collective-permute-start.35 = (bf16[384,1024]{1,0:T(8,128)(2,1)S(1)}, bf16[384,1024]{1,0:T(8,128)(2,1)S(1)}, u32[]{:S(2)}, u32[]{:S(2)}) collective-permute-start(bf16[384,1024]{1,0:T(8,128)(2,1)S(1)} %get-tuple-element.169), channel_id=1, source_target_pairs={{0,2},{1,3},{6,4},{7,5},{8,10},{9,11},{14,12},{15,13},{16,18},{17,... | collective-permute-start | bytes 2359304 | tf_op jit(solution)/shard_map/ppermute | solution.py:596
  259.6 18.6 %collective-permute-start.34 = (bf16[1,384,1024]{2,1,0:T(8,128)(2,1)}, bf16[1,384,1024]{2,1,0:T(8,128)(2,1)}, u32[]{:S(2)}, u32[]{:S(2)}) collective-permute-start(bf16[1,384,1024]{2,1,0:T(8,128)(2,1)} %get-tuple-element.168), channel_id=1, source_target_pairs={{0,1},{1,0},{2,3},{3,2},{4,5},{5,4},{6,7},{7,6},{8,9},{9,8},{10,11... | collective-permute-start | bytes 2359304 | tf_op jit(solution)/shard_map/ppermute | solution.py:530
  263.0 34.1 %collective-permute-start.31 = (bf16[384,1024]{1,0:T(8,128)(2,1)}, bf16[384,1024]{1,0:T(8,128)(2,1)}, u32[]{:S(2)}, u32[]{:S(2)}) collective-permute-start(bf16[384,1024]{1,0:T(8,128)(2,1)} %get-tuple-element.162), channel_id=1, source_target_pairs={{0,2},{1,3},{2,4},{3,5},{4,6},{5,7},{8,10},{9,11},{10,12},{11,13},... | collective-permute-start | bytes 2359304 | tf_op jit(solution)/shard_map/ppermute | solution.py:598
  265.5 33.6 %collective-permute-start.32 = (bf16[384,1024]{1,0:T(8,128)(2,1)}, bf16[384,1024]{1,0:T(8,128)(2,1)}, u32[]{:S(2)}, u32[]{:S(2)}) collective-permute-start(bf16[384,1024]{1,0:T(8,128)(2,1)} %get-tuple-element.163), channel_id=1, source_target_pairs={{2,0},{3,1},{4,2},{5,3},{6,4},{7,5},{10,8},{11,9},{12,10},{13,11},... | collective-permute-start | bytes 2359304 | tf_op jit(solution)/shard_map/ppermute | solution.py:598
  280.9 21.8 %collective-permute-start.37 = (bf16[384,1024]{1,0:T(8,128)(2,1)S(1)}, bf16[384,1024]{1,0:T(8,128)(2,1)S(1)}, u32[]{:S(2)}, u32[]{:S(2)}) collective-permute-start(bf16[384,1024]{1,0:T(8,128)(2,1)S(1)} %get-tuple-element.177), channel_id=1, source_target_pairs={{0,2},{1,3},{2,4},{3,5},{8,10},{9,11},{10,12},{11,13},{16,18},{17,... | collective-permute-start | bytes 2359304 | tf_op jit(solution)/shard_map/ppermute | solution.py:598
  285.6 17.1 %collective-permute-start.38 = (bf16[384,1024]{1,0:T(8,128)(2,1)S(1)}, bf16[384,1024]{1,0:T(8,128)(2,1)S(1)}, u32[]{:S(2)}, u32[]{:S(2)}) collective-permute-start(bf16[384,1024]{1,0:T(8,128)(2,1)S(1)} %get-tuple-element.178), channel_id=1, source_target_pairs={{4,2},{5,3},{6,4},{7,5},{12,10},{13,11},{14,12},{15,13},{20,18},{2... | collective-permute-start | bytes 2359304 | tf_op jit(solution)/shard_map/ppermute | solution.py:598
  310.4 19.6 %collective-permute-start.45 = (bf16[3,64,1024]{2,1,0:T(8,128)(2,1)S(1)}, bf16[3,64,1024]{2,1,0:T(8,128)(2,1)}, u32[]{:S(2)}, u32[]{:S(2)}) collective-permute-start(bf16[3,64,1024]{2,1,0:T(8,128)(2,1)S(1)} %get-tuple-element.192), channel_id=1, source_target_pairs={{0,8},{8,0},{16,24},{24,16},{1,9},{9,1},{17,25},{25,17},{2,10},{10... | collective-permute-start | bytes 1179656 | tf_op jit(solution)/shard_map/ppermute | solution.py:629
  314.2 19.8 %collective-permute-start.43 = (bf16[384,1024]{1,0:T(8,128)(2,1)}, bf16[384,1024]{1,0:T(8,128)(2,1)S(1)}, u32[]{:S(2)}, u32[]{:S(2)}) collective-permute-start(bf16[384,1024]{1,0:T(8,128)(2,1)} %get-tuple-element.188), channel_id=1, source_target_pairs={{0,2},{1,3},{2,4},{3,5},{4,6},{5,7},{8,10},{9,11},{10,12},{11,13},... | collective-permute-start | bytes 2359304 | tf_op jit(solution)/shard_map/ppermute | solution.py:598
  317.8 21.1 %collective-permute-start.44 = (bf16[384,1024]{1,0:T(8,128)(2,1)}, bf16[384,1024]{1,0:T(8,128)(2,1)S(1)}, u32[]{:S(2)}, u32[]{:S(2)}) collective-permute-start(bf16[384,1024]{1,0:T(8,128)(2,1)} %get-tuple-element.189), channel_id=1, source_target_pairs={{2,0},{3,1},{4,2},{5,3},{6,4},{7,5},{10,8},{11,9},{12,10},{13,11},... | collective-permute-start | bytes 2359304 | tf_op jit(solution)/shard_map/ppermute | solution.py:598
  (80 other events, 498.8 us)
Sparse Core Ops, SparseCore 0:
  39.4 33.1 reduce-scatter.6
  75.6 40.6 reduce-scatter.8
  212.2 41.0 all-gather.1

commit v3 on v2

--- a/solution.py
+++ b/solution.py
@@ -665,7 +665,7 @@
         if j == last - 1:
             hop = last_hop(mine, chips)
         shards += [mine, swap_cores(mine, chips)]
-        if j in (half - 1, last - 1):
+        if j == half - 1:
             *sums, mark = forward_part(
                 order[2 * begun : 2 * j + 2], shards, gate_weight, up_weight, sums, [mark]
             )

time: 353 us -> 352 us (level)
  waiting for transfers between devices: 41.3 us -> 57.6 us
  Pallas kernels: 175 us -> 164 us
    ppermute x2, waiting for transfers between devices: 3.72 us -> 15.6 us  [last_hop(): lax.ppermute(shard, 'tensor', line_pairs([chips - 2], 1) + line_pairs([1]...]
    pallas_call x39 -> x38, Pallas kernels: 175 us -> 164 us  [ordered_call(): return lambda *operands: call(*(place(x) for x in operands), *after)]
    unnamed x5, waiting for transfers between devices: 0.75 us -> 5.27 us
    unnamed x126 -> x132, local copies, waits for them, and re-layouts: 41.2 us -> 38.4 us
  transfers between devices with their start and end apart: 49 -> 49, of which waited for: 18 -> 19; matrix products, arithmetic and copies ran while one was open for 3% -> 3% of each run, Pallas kernels for 44% -> 41%
where the time goes in v3:
time: 352 us; the launch traced here: 351 us
  Pallas kernels  164 us (47%)
  starting transfers between devices  66.1 us (19%)
  waiting for transfers between devices  57.6 us (16%)
  local copies, waits for them, and re-layouts  44.1 us (13%)
  between operations  14.7 us (4%)
  other arithmetic  3.94 us (1%)
    pallas_call x38, Pallas kernels, ordered_call(): return lambda *operands: call(*(place(x) for x in operands), *after)  164 us
    unnamed x132, local copies, waits for them, and re-layouts  38.4 us
    ppermute x2, waiting for transfers between devices, last_hop(): lax.ppermute(shard, 'tensor', line_pairs([chips - 2], 1) + line_pairs([1]...  15.6 us
    ppermute x4, starting transfers between devices, scatter_hop(): lax.ppermute(payload[0], 'tensor', up)  14.4 us
    ppermute x2, starting transfers between devices, scatter_hop(): both = lax.ppermute(payload[0], 'tensor', up + down)  12.2 us
    ppermute x4, waiting for transfers between devices, scatter_hop(): lax.ppermute(payload[0], 'tensor', up)  9.47 us
    ppermute x7, starting transfers between devices, from_distance(): return lax.ppermute(x, 'tensor', [(i, i ^ distance) for i in range(size)])  9.23 us
    ppermute x4, starting transfers between devices, line_hop(): lax.ppermute(left, 'tensor', line_pairs(range(s - 1, chips - 1), 1))  8.36 us
  transfers between devices with their start and end apart: 49, of which 19 were waited for; matrix products, arithmetic and copies ran while one was open for 3% of the time, Pallas kernels for 41%

profile of v3, /device:TPU:0, one launch (start us, length us, event | category | flops | bytes accessed | tf_op | source)
XLA Modules:
  0.0 350.7 jit_solution(2331098024982320996)
XLA Ops:
  8.5 5.6 %collective-permute-start.2 = (bf16[384,1024]{1,0:T(8,128)(2,1)}, bf16[384,1024]{1,0:T(8,128)(2,1)S(1)}, u32[]{:S(2)}, u32[]{:S(2)}) collective-permute-start(bf16[384,1024]{1,0:T(8,128)(2,1)} %refs_1_.5), channel_id=1, source_target_pairs={{0,2},{1,3},{2,4},{3,5},{4,6},{5,7},{8,10},{9,11},{10,12},{11,13},... | collective-permute-start | bytes 2359304 | tf_op jit(solution)/shard_map/ppermute | solution.py:543
  22.4 7.5 %collective-permute-done.refs_1_.refs_3_ = bf16[384,1024]{1,0:T(8,128)(2,1)S(1)} collective-permute-done((bf16[384,1024]{1,0:T(8,128)(2,1)}, bf16[384,1024]{1,0:T(8,128)(2,1)S(1)}, u32[]{:S(2)}, u32[]{:S(2)}) %collective-permute-start) | collective-permute-done | bytes 786464 | tf_op jit(solution)/shard_map/ppermute | solution.py:544
  44.8 18.3 %forward_part.2 = (f32[384,1792]{1,0:T(8,128)S(1)}, f32[384,1792]{1,0:T(8,128)S(1)}, f32[8,128]{1,0:T(8,128)S(1)}) custom-call(s32[4]{0:T(128)S(1)} %slice.55.refs_0_, bf16[384,1024]{1,0:T(8,128)(2,1)S(1)} %copy-done.17, bf16[384,1024]{1,0:T(8,128)(2,1)} %collective-permute-done.4.refs_2_, bf16[384,1024]{1,0:T(8,128)(2,1)S(1)} %get-tuple-element.98.refs_3_, ...), custom_call_target="tpu_custom_call" | custom-call | flops 11274289152 | bytes 29360128 | tf_op jit(solution)/shard_map/forward_part/pallas_call | solution.py:57
  68.3 4.5 %reduce-scatter.7.cloned.1.call-done.refs_1_.refs_2_ = bf16[3,64,1024]{2,1,0:T(8,128)(2,1)} async-done(((bf16[12,64,1024]{2,1,0:T(8,128)(2,1)}), bf16[3,64,1024]{2,1,0:T(8,128)(2,1)}) %reduce-scatter.7.cloned.1.call-update) | async-done | bytes 393232
  76.9 14.7 %collective-permute-done.9.refs_1_ = bf16[384,1024]{1,0:T(8,128)(2,1)} collective-permute-done((bf16[384,1024]{1,0:T(8,128)(2,1)S(1)}, bf16[384,1024]{1,0:T(8,128)(2,1)}, u32[]{:S(2)}, u32[]{:S(2)}) %collective-permute-start.9) | collective-permute-done | bytes 786464 | tf_op jit(solution)/shard_map/ppermute | solution.py:549
  91.7 2.6 copy_chosen.8
  105.6 17.7 %forward_part.3 = (f32[384,1792]{1,0:T(8,128)S(1)}, f32[384,1792]{1,0:T(8,128)S(1)}, f32[8,128]{1,0:T(8,128)S(1)}) custom-call(s32[4]{0:T(128)S(1)} %slice.53.refs_0_, bf16[384,1024]{1,0:T(8,128)(2,1)S(1)} %get-tuple-element.102.refs_1_, bf16[384,1024]{1,0:T(8,128)(2,1)} %collective-permute-done.8.refs_2_, bf16[384,1024]{1,0:T(8,128)(2,1)} %get-tuple-element.109.refs_3_, ...), custom_call_target="tpu_custom_call" | custom-call | flops 11274289152 | bytes 29360128 | tf_op jit(solution)/shard_map/forward_part/pallas_call | solution.py:57
  131.8 4.9 %activate.1 = (bf16[384,1792]{1,0:T(8,128)(2,1)S(1)}, f32[384,1792]{1,0:T(8,128)}, f32[384,1792]{1,0:T(8,128)}, f32[8,128]{1,0:T(8,128)S(1)}) custom-call(f32[384,1792]{1,0:T(8,128)S(1)} %copy-done.50, f32[384,1792]{1,0:T(8,128)S(1)} %copy-done.52, bf16[384,64]{1,0:T(8,128)(2,1)S(1)} %multiply_convert_fusion.refs_2_.refs_12_, ...), custom_call_target="tpu_custom_call" | custom-call | flops 2147483648 | bytes 5592405 | tf_op jit(solution)/shard_map/activate/pallas_call | solution.py:57
  139.9 5.9 %mixed_parts.2 = (bf16[1,384,1024]{2,1,0:T(8,128)(2,1)S(1)}, bf16[1,384,1024]{2,1,0:T(8,128)(2,1)S(1)}, f32[8,128]{1,0:T(8,128)S(1)}) custom-call(s32[2]{0:T(128)S(1)} %get-tuple-element.195.refs_0_, bf16[384,1792]{1,0:T(8,128)(2,1)S(1)} %get-tuple-element.119.refs_1_, bf16[1792,8192]{1,0:T(8,128)(2,1)} %refs_8_.7, bf16[1792,8192]{1,0:T(8,128)(2,1)} %refs_8_.7, ...), custom_call_target="tpu_custom_call" | custom-call | flops 2818572288 | bytes 7340032 | tf_op jit(solution)/shard_map/mixed_parts/pallas_call | solution.py:57
  145.9 13.6 %mixed_parts.3 = (bf16[3,384,1024]{2,1,0:T(8,128)(2,1)S(1)}, bf16[3,384,1024]{2,1,0:T(8,128)(2,1)S(1)}, f32[8,128]{1,0:T(8,128)S(1)}) custom-call(s32[6]{0:T(128)S(1)} %slice.51.refs_0_, bf16[384,1792]{1,0:T(8,128)(2,1)S(1)} %get-tuple-element.119.refs_1_, bf16[1792,8192]{1,0:T(8,128)(2,1)} %refs_8_.7, bf16[1792,8192]{1,0:T(8,128)(2,1)} %refs_8_.7, ...), custom_call_target="tpu_custom_call" | custom-call | flops 8455716864 | bytes 22020096 | tf_op jit(solution)/shard_map/mixed_parts/pallas_call | solution.py:57
  166.4 9.1 %collective-permute-start.21 = (bf16[384,1024]{1,0:T(8,128)(2,1)S(1)}, bf16[384,1024]{1,0:T(8,128)(2,1)S(1)}, u32[]{:S(2)}, u32[]{:S(2)}) collective-permute-start(bf16[384,1024]{1,0:T(8,128)(2,1)S(1)} %get-tuple-element.133), channel_id=1, source_target_pairs={{0,2},{1,3},{6,4},{7,5},{8,10},{9,11},{14,12},{15,13},{16,18},{17,... | collective-permute-start | bytes 2359304 | tf_op jit(solution)/shard_map/ppermute | solution.py:596
  175.5 12.1 %hidden_part.1 = (f32[384,1792]{1,0:T(8,128)}, f32[8,128]{1,0:T(8,128)S(1)}) custom-call(s32[4]{0:T(128)S(1)} %slice.55.refs_0_, bf16[384,1024]{1,0:T(8,128)(2,1)S(1)} %copy-done.33, bf16[384,1024]{1,0:T(8,128)(2,1)S(1)} %collective-permute-done.23.refs_2_, bf16[384,1024]{1,0:T(8,128)(2,1)S(1)} %get-tuple-element.135.refs_3_, ...), custom_call_target="tpu_custom_call" | custom-call | flops 5637144576 | bytes 14680064 | tf_op jit(solution)/shard_map/hidden_part/pallas_call | solution.py:57
  194.8 14.0 %hidden_gradients.1 = (bf16[384,1792]{1,0:T(8,128)(2,1)S(1)}, bf16[384,1792]{1,0:T(8,128)(2,1)S(1)}, f32[384,64]{1,0:T(8,128)S(1)}, bf16[3,64,1792]{2,1,0:T(8,128)(2,1)S(1)}, f32[8,128]{1,0:T(8,128)S(1)}) custom-call(s32[4]{0:T(128)S(1)} %slice.53.refs_0_, bf16[384,1024]{1,0:T(8,128)(2,1)S(1)} %get-tuple-element.134.refs_1_, ...), custom_call_target="tpu_custom_call" | custom-call | flops 5637144576 | bytes 14680064 | tf_op jit(solution)/shard_map/hidden_gradients/pallas_call | solution.py:57
  216.0 6.3 %item_part.5 = (bf16[1,384,1024]{2,1,0:T(8,128)(2,1)S(1)}, f32[8,128]{1,0:T(8,128)S(1)}) custom-call(s32[1]{0:T(128)} %get-tuple-element.210.refs_0_, bf16[384,1792]{1,0:T(8,128)(2,1)S(1)} %copy-done.4, bf16[384,1792]{1,0:T(8,128)(2,1)S(1)} %copy-done.8, bf16[8192,1792]{1,0:T(8,128)(2,1)} %refs_5_.13, bf16[8192,1792]{1,0:T(8,128)(2,1)} %refs_6_.13, ...), custom_call_target="tpu_custom_call" | custom-call | flops 2818572288 | bytes 7340032 | tf_op jit(solution)/shard_map/item_part/pallas_call | solution.py:57
  222.4 4.5 %collective-permute-start.25 = (bf16[384,1024]{1,0:T(8,128)(2,1)S(1)}, bf16[384,1024]{1,0:T(8,128)(2,1)S(1)}, u32[]{:S(2)}, u32[]{:S(2)}) collective-permute-start(bf16[384,1024]{1,0:T(8,128)(2,1)S(1)} %copy-done.58), channel_id=1, source_target_pairs={{0,2},{1,3},{2,4},{3,5},{8,10},{9,11},{10,12},{11,13},{16,18},{17,... | collective-permute-start | bytes 2359304 | tf_op jit(solution)/shard_map/ppermute | solution.py:598
  230.1 6.3 %item_part.6 = (bf16[1,384,1024]{2,1,0:T(8,128)(2,1)S(1)}, f32[8,128]{1,0:T(8,128)S(1)}) custom-call(s32[1]{0:T(128)} %get-tuple-element.211.refs_0_, bf16[384,1792]{1,0:T(8,128)(2,1)S(1)} %copy-done.5, bf16[384,1792]{1,0:T(8,128)(2,1)S(1)} %copy-done.8, bf16[8192,1792]{1,0:T(8,128)(2,1)} %refs_5_.13, bf16[8192,1792]{1,0:T(8,128)(2,1)} %refs_6_.13, ...), custom_call_target="tpu_custom_call" | custom-call | flops 2818572288 | bytes 7340032 | tf_op jit(solution)/shard_map/item_part/pallas_call | solution.py:57
  237.3 3.1 collective-permute-start.35
  240.4 4.3 %collective-permute-done.25.refs_9_ = bf16[384,1024]{1,0:T(8,128)(2,1)S(1)} collective-permute-done((bf16[384,1024]{1,0:T(8,128)(2,1)S(1)}, bf16[384,1024]{1,0:T(8,128)(2,1)S(1)}, u32[]{:S(2)}, u32[]{:S(2)}) %collective-permute-start.25) | collective-permute-done | bytes 786464 | tf_op jit(solution)/shard_map/ppermute | solution.py:598
  249.0 10.6 %item_part.7 = (bf16[1,384,1024]{2,1,0:T(8,128)(2,1)S(1)}, bf16[1,384,1024]{2,1,0:T(8,128)(2,1)}, f32[8,128]{1,0:T(8,128)S(1)}) custom-call(s32[2]{0:T(128)S(1)} %get-tuple-element.193.refs_0_, bf16[384,1792]{1,0:T(8,128)(2,1)S(1)} %copy-done.5, bf16[384,1792]{1,0:T(8,128)(2,1)S(1)} %copy-done.9, bf16[8192,1792]{1,0:T(8,128)(2,1)} %refs_5_.13, ...), custom_call_target="tpu_custom_call" | custom-call | flops 5637144576 | bytes 14680064 | tf_op jit(solution)/shard_map/item_part/pallas_call | solution.py:57
  260.2 3.6 %collective-permute-start.36 = (f32[384,64]{1,0:T(8,128)S(1)}, f32[384,64]{1,0:T(8,128)S(1)}, u32[]{:S(2)}, u32[]{:S(2)}) collective-permute-start(f32[384,64]{1,0:T(8,128)S(1)} %get-tuple-element.164.refs_3_), channel_id=1, source_target_pairs={{0,4},{1,5},{2,6},{3,7},{4,0},{5,1},{6,2},{7,3},{8,12},{9,13},{10,... | collective-permute-start | bytes 294920 | tf_op jit(solution)/shard_map/ppermute | solution.py:632
  271.9 3.3 slot_sums.2
  279.1 2.7 line_sums.12
  281.8 4.6 %collective-permute-start.37 = (bf16[384,1024]{1,0:T(8,128)(2,1)S(1)}, bf16[384,1024]{1,0:T(8,128)(2,1)S(1)}, u32[]{:S(2)}, u32[]{:S(2)}) collective-permute-start(bf16[384,1024]{1,0:T(8,128)(2,1)S(1)} %get-tuple-element.171), channel_id=1, source_target_pairs={{0,2},{1,3},{2,4},{3,5},{8,10},{9,11},{10,12},{11,13},{16,18},{17,... | collective-permute-start | bytes 2359304 | tf_op jit(solution)/shard_map/ppermute | solution.py:598
  287.2 10.1 %item_part.8 = (bf16[1,384,1024]{2,1,0:T(8,128)(2,1)S(1)}, bf16[1,384,1024]{2,1,0:T(8,128)(2,1)S(1)}, f32[8,128]{1,0:T(8,128)S(1)}) custom-call(s32[2]{0:T(128)S(1)} %get-tuple-element.194.refs_0_, bf16[384,1792]{1,0:T(8,128)(2,1)S(1)} %copy-done.6, bf16[384,1792]{1,0:T(8,128)(2,1)S(1)} %copy-done.10, bf16[8192,1792]{1,0:T(8,128)(2,1)} %refs_5_.13, ...), custom_call_target="tpu_custom_call" | custom-call | flops 5637144576 | bytes 14680064 | tf_op jit(solution)/shard_map/item_part/pallas_call | solution.py:57
  303.3 2.9 line_sums.13
  306.2 3.3 collective-permute-done.40.refs_0_
  311.4 3.3 line_sums.14
  314.7 3.0 collective-permute-start.43
  319.0 10.6 %item_part.9 = (bf16[1,384,1024]{2,1,0:T(8,128)(2,1)S(1)}, bf16[1,384,1024]{2,1,0:T(8,128)(2,1)}, f32[8,128]{1,0:T(8,128)S(1)}) custom-call(s32[2]{0:T(128)S(1)} %get-tuple-element.192.refs_0_, bf16[384,1792]{1,0:T(8,128)(2,1)S(1)} %copy-done.6, bf16[384,1792]{1,0:T(8,128)(2,1)S(1)} %copy-done.10, bf16[8192,1792]{1,0:T(8,128)(2,1)} %refs_5_.13, ...), custom_call_target="tpu_custom_call" | custom-call | flops 5637144576 | bytes 14680064 | tf_op jit(solution)/shard_map/item_part/pallas_call | solution.py:57
  331.0 2.8 collective-permute-done.43.refs_3_
  333.8 4.9 %collective-permute-done.44.refs_4_ = bf16[384,1024]{1,0:T(8,128)(2,1)S(1)} collective-permute-done((bf16[384,1024]{1,0:T(8,128)(2,1)}, bf16[384,1024]{1,0:T(8,128)(2,1)S(1)}, u32[]{:S(2)}, u32[]{:S(2)}) %collective-permute-start.44) | collective-permute-done | bytes 786464 | tf_op jit(solution)/shard_map/ppermute | solution.py:598
  341.1 3.0 line_sums.15
  (271 shorter events, 112.1 us)
Async XLA Ops:
  7.2 65.7 %reduce-scatter.7.cloned.1.call-start = ((), (), s32[]{:S(2)}) async-start(), calls=%async_computation.3 | async-start | bytes 1966080
  7.2 22.7 %collective-permute-start = (bf16[384,1024]{1,0:T(8,128)(2,1)}, bf16[384,1024]{1,0:T(8,128)(2,1)S(1)}, u32[]{:S(2)}, u32[]{:S(2)}) collective-permute-start(bf16[384,1024]{1,0:T(8,128)(2,1)} %refs_1_.5), channel_id=1, source_target_pairs={{2,0},{3,1},{4,2},{5,3},{6,4},{7,5},{10,8},{11,9},{12,10},{13,11},... | collective-permute-start | bytes 2359304 | tf_op jit(solution)/shard_map/ppermute | solution.py:544
  8.5 22.7 %collective-permute-start.2 = (bf16[384,1024]{1,0:T(8,128)(2,1)}, bf16[384,1024]{1,0:T(8,128)(2,1)S(1)}, u32[]{:S(2)}, u32[]{:S(2)}) collective-permute-start(bf16[384,1024]{1,0:T(8,128)(2,1)} %refs_1_.5), channel_id=1, source_target_pairs={{0,2},{1,3},{2,4},{3,5},{4,6},{5,7},{8,10},{9,11},{10,12},{11,13},... | collective-permute-start | bytes 2359304 | tf_op jit(solution)/shard_map/ppermute | solution.py:543
  39.5 87.7 %reduce-scatter.9.cloned.1.call-start = ((), (), s32[]{:S(2)}) async-start(), calls=%async_computation.4 | async-start | bytes 3440640
  40.2 228.1 %all-gather.2.cloned.1.call-start = ((), (), s32[]{:S(2)}) async-start(), calls=%async_computation.2 | async-start | bytes 3440640 | tf_op jit(solution)/shard_map/all_gather | solution.py:723
  42.7 23.4 %collective-permute-start.1 = (bf16[384,1024]{1,0:T(8,128)(2,1)S(1)}, bf16[384,1024]{1,0:T(8,128)(2,1)S(1)}, u32[]{:S(2)}, u32[]{:S(2)}) collective-permute-start(bf16[384,1024]{1,0:T(8,128)(2,1)S(1)} %collective-permute-done.refs_1_.refs_3_), channel_id=1, source_target_pairs={{2,0},{3,1},{4,2},{5,3},{10,8},{11,9},{12,10},{13,11},{18,16},{19,... | collective-permute-start | bytes 2359304 | tf_op jit(solution)/shard_map/ppermute | solution.py:544
  44.0 22.1 %collective-permute-start.3 = (bf16[384,1024]{1,0:T(8,128)(2,1)S(1)}, bf16[384,1024]{1,0:T(8,128)(2,1)S(1)}, u32[]{:S(2)}, u32[]{:S(2)}) collective-permute-start(bf16[384,1024]{1,0:T(8,128)(2,1)S(1)} %collective-permute-done.2.refs_2_), channel_id=1, source_target_pairs={{2,4},{3,5},{4,6},{5,7},{10,12},{11,13},{12,14},{13,15},{18,20},{1... | collective-permute-start | bytes 2359304 | tf_op jit(solution)/shard_map/ppermute | solution.py:543
  67.0 24.7 %collective-permute-start.9 = (bf16[384,1024]{1,0:T(8,128)(2,1)S(1)}, bf16[384,1024]{1,0:T(8,128)(2,1)}, u32[]{:S(2)}, u32[]{:S(2)}) collective-permute-start(bf16[384,1024]{1,0:T(8,128)(2,1)S(1)} %get-tuple-element.102.refs_1_), channel_id=1, source_target_pairs={{4,6},{5,7},{2,0},{3,1},{12,14},{13,15},{10,8},{11,9},{20,22},{21,... | collective-permute-start | bytes 2359304 | tf_op jit(solution)/shard_map/ppermute | solution.py:549
  74.9 24.6 %collective-permute-start.8 = (bf16[384,1024]{1,0:T(8,128)(2,1)S(1)}, bf16[384,1024]{1,0:T(8,128)(2,1)}, u32[]{:S(2)}, u32[]{:S(2)}) collective-permute-start(bf16[384,1024]{1,0:T(8,128)(2,1)S(1)} %get-tuple-element.102.refs_1_), channel_id=1, source_target_pairs={{0,1},{1,0},{2,3},{3,2},{4,5},{5,4},{6,7},{7,6},{8,9},{9,8},{10,11... | collective-permute-start | bytes 2359304 | tf_op jit(solution)/shard_map/ppermute | solution.py:530
  95.0 31.4 %collective-permute-start.12 = (f32[384,64]{1,0:T(8,128)S(1)}, f32[384,64]{1,0:T(8,128)S(1)}, u32[]{:S(2)}, u32[]{:S(2)}) collective-permute-start(f32[384,64]{1,0:T(8,128)S(1)} %get-tuple-element.115.refs_0_), channel_id=1, source_target_pairs={{0,2},{1,3},{2,0},{3,1},{4,6},{5,7},{6,4},{7,5},{8,10},{9,11},{10,... | collective-permute-start | bytes 294920 | tf_op jit(solution)/shard_map/ppermute | solution.py:632
  95.0 31.3 %collective-permute-start.13 = (f32[384,64]{1,0:T(8,128)S(1)}, f32[384,64]{1,0:T(8,128)S(1)}, u32[]{:S(2)}, u32[]{:S(2)}) collective-permute-start(f32[384,64]{1,0:T(8,128)S(1)} %get-tuple-element.115.refs_0_), channel_id=1, source_target_pairs={{0,4},{1,5},{2,6},{3,7},{4,0},{5,1},{6,2},{7,3},{8,12},{9,13},{10,... | collective-permute-start | bytes 294920 | tf_op jit(solution)/shard_map/ppermute | solution.py:632
  97.1 29.3 %collective-permute-start.14 = (f32[384,64]{1,0:T(8,128)S(1)}, f32[384,64]{1,0:T(8,128)S(1)}, u32[]{:S(2)}, u32[]{:S(2)}) collective-permute-start(f32[384,64]{1,0:T(8,128)S(1)} %get-tuple-element.115.refs_0_), channel_id=1, source_target_pairs={{0,6},{1,7},{2,4},{3,5},{4,2},{5,3},{6,0},{7,1},{8,14},{9,15},{10,... | collective-permute-start | bytes 294920 | tf_op jit(solution)/shard_map/ppermute | solution.py:632
  99.4 37.3 %collective-permute-start.15 = (bf16[384,1024]{1,0:T(8,128)(2,1)S(1)}, bf16[384,1024]{1,0:T(8,128)(2,1)S(1)}, u32[]{:S(2)}, u32[]{:S(2)}) collective-permute-start(bf16[384,1024]{1,0:T(8,128)(2,1)S(1)} %get-tuple-element.120.refs_1_), channel_id=1, source_target_pairs={{0,2},{1,3},{2,4},{3,5},{4,6},{5,7},{8,10},{9,11},{10,12},{11,13},... | collective-permute-start | bytes 2359304 | tf_op jit(solution)/shard_map/ppermute | solution.py:543
  100.8 36.0 %collective-permute-start.16 = (bf16[384,1024]{1,0:T(8,128)(2,1)S(1)}, bf16[384,1024]{1,0:T(8,128)(2,1)}, u32[]{:S(2)}, u32[]{:S(2)}) collective-permute-start(bf16[384,1024]{1,0:T(8,128)(2,1)S(1)} %get-tuple-element.120.refs_1_), channel_id=1, source_target_pairs={{2,0},{3,1},{4,2},{5,3},{6,4},{7,5},{10,8},{11,9},{12,10},{13,11},... | collective-permute-start | bytes 2359304 | tf_op jit(solution)/shard_map/ppermute | solution.py:544
  137.9 23.1 %collective-permute-start.19 = (bf16[384,1024]{1,0:T(8,128)(2,1)S(1)}, bf16[384,1024]{1,0:T(8,128)(2,1)S(1)}, u32[]{:S(2)}, u32[]{:S(2)}) collective-permute-start(bf16[384,1024]{1,0:T(8,128)(2,1)S(1)} %get-tuple-element.128.refs_1_.refs_3_), channel_id=1, source_target_pairs={{2,0},{3,1},{4,2},{5,3},{10,8},{11,9},{12,10},{13,11},{18,16},{19,... | collective-permute-start | bytes 2359304 | tf_op jit(solution)/shard_map/ppermute | solution.py:544
  139.2 22.3 %collective-permute-start.20 = (bf16[384,1024]{1,0:T(8,128)(2,1)S(1)}, bf16[384,1024]{1,0:T(8,128)(2,1)S(1)}, u32[]{:S(2)}, u32[]{:S(2)}) collective-permute-start(bf16[384,1024]{1,0:T(8,128)(2,1)S(1)} %get-tuple-element.129.refs_2_), channel_id=1, source_target_pairs={{2,4},{3,5},{4,6},{5,7},{10,12},{11,13},{12,14},{13,15},{18,20},{1... | collective-permute-start | bytes 2359304 | tf_op jit(solution)/shard_map/ppermute | solution.py:543
  159.5 32.9 %collective-permute-start.17 = (bf16[3,384,1024]{2,1,0:T(8,128)(2,1)S(1)}, bf16[3,384,1024]{2,1,0:T(8,128)(2,1)S(1)}, u32[]{:S(2)}, u32[]{:S(2)}) collective-permute-start(bf16[3,384,1024]{2,1,0:T(8,128)(2,1)S(1)} %get-tuple-element.125), channel_id=1, source_target_pairs={{0,1},{1,0},{2,3},{3,2},{4,5},{5,4},{6,7},{7,6},{8,9},{9,8},{10,11... | collective-permute-start | bytes 7077896 | tf_op jit(solution)/shard_map/ppermute | solution.py:530
  162.3 26.0 %collective-permute-start.22 = (bf16[384,1024]{1,0:T(8,128)(2,1)S(1)}, bf16[384,1024]{1,0:T(8,128)(2,1)S(1)}, u32[]{:S(2)}, u32[]{:S(2)}) collective-permute-start(bf16[384,1024]{1,0:T(8,128)(2,1)S(1)} %get-tuple-element.134.refs_1_), channel_id=1, source_target_pairs={{4,6},{5,7},{2,0},{3,1},{12,14},{13,15},{10,8},{11,9},{20,22},{21,... | collective-permute-start | bytes 2359304 | tf_op jit(solution)/shard_map/ppermute | solution.py:549
  165.2 29.5 %collective-permute-start.27 = (bf16[384,1024]{1,0:T(8,128)(2,1)S(1)}, bf16[384,1024]{1,0:T(8,128)(2,1)S(1)}, u32[]{:S(2)}, u32[]{:S(2)}) collective-permute-start(bf16[384,1024]{1,0:T(8,128)(2,1)S(1)} %get-tuple-element.134.refs_1_), channel_id=1, source_target_pairs={{0,1},{1,0},{2,3},{3,2},{4,5},{5,4},{6,7},{7,6},{8,9},{9,8},{10,11... | collective-permute-start | bytes 2359304 | tf_op jit(solution)/shard_map/ppermute | solution.py:530
  166.4 26.0 %collective-permute-start.21 = (bf16[384,1024]{1,0:T(8,128)(2,1)S(1)}, bf16[384,1024]{1,0:T(8,128)(2,1)S(1)}, u32[]{:S(2)}, u32[]{:S(2)}) collective-permute-start(bf16[384,1024]{1,0:T(8,128)(2,1)S(1)} %get-tuple-element.133), channel_id=1, source_target_pairs={{0,2},{1,3},{6,4},{7,5},{8,10},{9,11},{14,12},{15,13},{16,18},{17,... | collective-permute-start | bytes 2359304 | tf_op jit(solution)/shard_map/ppermute | solution.py:596
  222.4 22.3 %collective-permute-start.25 = (bf16[384,1024]{1,0:T(8,128)(2,1)S(1)}, bf16[384,1024]{1,0:T(8,128)(2,1)S(1)}, u32[]{:S(2)}, u32[]{:S(2)}) collective-permute-start(bf16[384,1024]{1,0:T(8,128)(2,1)S(1)} %copy-done.58), channel_id=1, source_target_pairs={{0,2},{1,3},{2,4},{3,5},{8,10},{9,11},{10,12},{11,13},{16,18},{17,... | collective-permute-start | bytes 2359304 | tf_op jit(solution)/shard_map/ppermute | solution.py:598
  226.9 17.8 %collective-permute-start.26 = (bf16[384,1024]{1,0:T(8,128)(2,1)S(1)}, bf16[384,1024]{1,0:T(8,128)(2,1)S(1)}, u32[]{:S(2)}, u32[]{:S(2)}) collective-permute-start(bf16[384,1024]{1,0:T(8,128)(2,1)S(1)} %copy-done.56), channel_id=1, source_target_pairs={{4,2},{5,3},{6,4},{7,5},{12,10},{13,11},{14,12},{15,13},{20,18},{2... | collective-permute-start | bytes 2359304 | tf_op jit(solution)/shard_map/ppermute | solution.py:598
  229.2 19.7 %collective-permute-start.33 = (f32[384,64]{1,0:T(8,128)S(1)}, f32[384,64]{1,0:T(8,128)S(1)}, u32[]{:S(2)}, u32[]{:S(2)}) collective-permute-start(f32[384,64]{1,0:T(8,128)S(1)} %get-tuple-element.158.refs_0_), channel_id=1, source_target_pairs={{0,2},{1,3},{2,0},{3,1},{4,6},{5,7},{6,4},{7,5},{8,10},{9,11},{10,... | collective-permute-start | bytes 294920 | tf_op jit(solution)/shard_map/ppermute | solution.py:632
  237.3 30.1 %collective-permute-start.35 = (bf16[384,1024]{1,0:T(8,128)(2,1)S(1)}, bf16[384,1024]{1,0:T(8,128)(2,1)S(1)}, u32[]{:S(2)}, u32[]{:S(2)}) collective-permute-start(bf16[384,1024]{1,0:T(8,128)(2,1)S(1)} %get-tuple-element.163), channel_id=1, source_target_pairs={{0,2},{1,3},{6,4},{7,5},{8,10},{9,11},{14,12},{15,13},{16,18},{17,... | collective-permute-start | bytes 2359304 | tf_op jit(solution)/shard_map/ppermute | solution.py:596
  260.2 18.9 %collective-permute-start.34 = (bf16[1,384,1024]{2,1,0:T(8,128)(2,1)}, bf16[1,384,1024]{2,1,0:T(8,128)(2,1)}, u32[]{:S(2)}, u32[]{:S(2)}) collective-permute-start(bf16[1,384,1024]{2,1,0:T(8,128)(2,1)} %get-tuple-element.162), channel_id=1, source_target_pairs={{0,1},{1,0},{2,3},{3,2},{4,5},{5,4},{6,7},{7,6},{8,9},{9,8},{10,11... | collective-permute-start | bytes 2359304 | tf_op jit(solution)/shard_map/ppermute | solution.py:530
  263.8 34.3 %collective-permute-start.31 = (bf16[384,1024]{1,0:T(8,128)(2,1)}, bf16[384,1024]{1,0:T(8,128)(2,1)}, u32[]{:S(2)}, u32[]{:S(2)}) collective-permute-start(bf16[384,1024]{1,0:T(8,128)(2,1)} %get-tuple-element.156), channel_id=1, source_target_pairs={{0,2},{1,3},{2,4},{3,5},{4,6},{5,7},{8,10},{9,11},{10,12},{11,13},... | collective-permute-start | bytes 2359304 | tf_op jit(solution)/shard_map/ppermute | solution.py:598
  266.1 33.4 %collective-permute-start.32 = (bf16[384,1024]{1,0:T(8,128)(2,1)}, bf16[384,1024]{1,0:T(8,128)(2,1)}, u32[]{:S(2)}, u32[]{:S(2)}) collective-permute-start(bf16[384,1024]{1,0:T(8,128)(2,1)} %get-tuple-element.157), channel_id=1, source_target_pairs={{2,0},{3,1},{4,2},{5,3},{6,4},{7,5},{10,8},{11,9},{12,10},{13,11},... | collective-permute-start | bytes 2359304 | tf_op jit(solution)/shard_map/ppermute | solution.py:598
  281.8 21.5 %collective-permute-start.37 = (bf16[384,1024]{1,0:T(8,128)(2,1)S(1)}, bf16[384,1024]{1,0:T(8,128)(2,1)S(1)}, u32[]{:S(2)}, u32[]{:S(2)}) collective-permute-start(bf16[384,1024]{1,0:T(8,128)(2,1)S(1)} %get-tuple-element.171), channel_id=1, source_target_pairs={{0,2},{1,3},{2,4},{3,5},{8,10},{9,11},{10,12},{11,13},{16,18},{17,... | collective-permute-start | bytes 2359304 | tf_op jit(solution)/shard_map/ppermute | solution.py:598
  286.4 16.9 %collective-permute-start.38 = (bf16[384,1024]{1,0:T(8,128)(2,1)S(1)}, bf16[384,1024]{1,0:T(8,128)(2,1)S(1)}, u32[]{:S(2)}, u32[]{:S(2)}) collective-permute-start(bf16[384,1024]{1,0:T(8,128)(2,1)S(1)} %get-tuple-element.172), channel_id=1, source_target_pairs={{4,2},{5,3},{6,4},{7,5},{12,10},{13,11},{14,12},{15,13},{20,18},{2... | collective-permute-start | bytes 2359304 | tf_op jit(solution)/shard_map/ppermute | solution.py:598
  310.8 19.0 %collective-permute-start.45 = (bf16[3,64,1024]{2,1,0:T(8,128)(2,1)S(1)}, bf16[3,64,1024]{2,1,0:T(8,128)(2,1)}, u32[]{:S(2)}, u32[]{:S(2)}) collective-permute-start(bf16[3,64,1024]{2,1,0:T(8,128)(2,1)S(1)} %get-tuple-element.186), channel_id=1, source_target_pairs={{0,8},{8,0},{16,24},{24,16},{1,9},{9,1},{17,25},{25,17},{2,10},{10... | collective-permute-start | bytes 1179656 | tf_op jit(solution)/shard_map/ppermute | solution.py:629
  314.7 19.1 %collective-permute-start.43 = (bf16[384,1024]{1,0:T(8,128)(2,1)}, bf16[384,1024]{1,0:T(8,128)(2,1)S(1)}, u32[]{:S(2)}, u32[]{:S(2)}) collective-permute-start(bf16[384,1024]{1,0:T(8,128)(2,1)} %get-tuple-element.182), channel_id=1, source_target_pairs={{0,2},{1,3},{2,4},{3,5},{4,6},{5,7},{8,10},{9,11},{10,12},{11,13},... | collective-permute-start | bytes 2359304 | tf_op jit(solution)/shard_map/ppermute | solution.py:598
  317.7 21.0 %collective-permute-start.44 = (bf16[384,1024]{1,0:T(8,128)(2,1)}, bf16[384,1024]{1,0:T(8,128)(2,1)S(1)}, u32[]{:S(2)}, u32[]{:S(2)}) collective-permute-start(bf16[384,1024]{1,0:T(8,128)(2,1)} %get-tuple-element.183), channel_id=1, source_target_pairs={{2,0},{3,1},{4,2},{5,3},{6,4},{7,5},{10,8},{11,9},{12,10},{13,11},... | collective-permute-start | bytes 2359304 | tf_op jit(solution)/shard_map/ppermute | solution.py:598
  (83 other events, 657.2 us)
Sparse Core Ops, SparseCore 0:
  39.6 33.1 reduce-scatter.6
  75.8 40.6 reduce-scatter.8
  212.7 41.1 all-gather.1
